TPU v7x, 32 devices: a whole 2x2x4 slice. The times are simulated.
32 devices in a mesh: seq: 8 (over z, y), head: 4 (over x, core).
Axes of the slice: x: 2, y: 2, z: 4, core: 2. Of those that a mesh axis runs over, the one named last changes fastest.
Arguments:
- tokens: bfloat16 [8192, 4096], P('seq'), may hold values from -50 to 50
- norm_gain: float32 [4096], replicated, may hold values from 0.1 to 1.9
- wq: bfloat16 [4096, 4096], P('seq', 'head'), may hold values from -2.34375 to 2.34375
- wk: bfloat16 [4096, 1024], P('seq', 'head'), may hold values from -0.09375 to 0.09375
- wv: bfloat16 [4096, 1024], P('seq', 'head'), may hold values from -0.09375 to 0.09375
- wo: bfloat16 [4096, 4096], P('head', 'seq'), may hold values from -0.125 to 0.125
- gate_bias: float32 [32], P('head'), may hold values from -3 to 3
- mem_init: float32 [8, 128, 128], P('head'), may hold values from -32768 to 32768
- norm_init: float32 [8, 128], P('head'), may hold values from 512 to 2048
Outputs:
- attended: bfloat16 [8192, 4096], P('seq', 'head')
All inputs are finite; a program needn't handle non-finite values.
Results may differ from a plain program's by a relative error of at most 0.018.
Values may be sent and summed in bfloat16 or wider, within the bound.
A program may use at most 128 MiB of HBM per device.

v0:
```python
import math

import jax
import jax.numpy as jnp
from jax import lax
from jax.sharding import PartitionSpec as P

H = 32
KVH = 8
HD = 128
SEG = 512


def from_behind(block, axis, distance):
    devices = range(lax.axis_size(axis))
    route = [(i - distance, i) for i in devices if i - distance in devices]
    return lax.ppermute(block, axis, route)


def feature_map(values_in):
    return jnp.where(values_in > 0, values_in + 1.0, jnp.exp(jnp.minimum(values_in, 0.0)))


def per_device(tokens, norm_gain, wq, wk, wv, wo, gate_bias, mem_init, norm_init):
    highest = lax.Precision.HIGHEST
    widened = tokens.astype(jnp.float32)
    normed = (
        widened * lax.rsqrt(jnp.mean(widened * widened, axis=-1, keepdims=True) + 1e-05) * norm_gain
    ).astype(jnp.bfloat16)
    token_count = normed.shape[0]

    def project(shard_piece):
        return jnp.dot(normed, shard_piece, preferred_element_type=jnp.float32)

    query_wide = project(lax.all_gather(wq, "seq", axis=0, tiled=True))
    key_wide = project(lax.all_gather(wk, "seq", axis=0, tiled=True))
    value_wide = project(lax.all_gather(wv, "seq", axis=0, tiled=True))
    queries = query_wide.astype(jnp.bfloat16)
    keys_all = key_wide.astype(jnp.bfloat16)
    values_all = value_wide.astype(jnp.bfloat16)
    group = H // KVH
    kv_local = wk.shape[1] // HD
    segments = token_count // SEG
    query_seg = queries.reshape(segments, SEG, kv_local, group, HD)
    key_seg = keys_all.reshape(segments, SEG, kv_local, HD)
    value_seg = values_all.reshape(segments, SEG, kv_local, HD)
    key_feats = feature_map(key_seg.astype(jnp.float32))
    delta_mem = jnp.einsum(
        "nski,nskj->nkij", key_feats, value_seg.astype(jnp.float32), precision=highest
    )
    delta_norm = jnp.sum(key_feats, axis=1)
    own_mem = jnp.sum(delta_mem, axis=0)
    own_norm = jnp.sum(delta_norm, axis=0)
    zero_mem = jnp.zeros_like(own_mem)
    zero_norm = jnp.zeros_like(own_norm)

    def pass_along(step_index, carried):
        return (
            from_behind((carried[0] + own_mem).astype(jnp.bfloat16), "seq", 1).astype(jnp.float32),
            from_behind((carried[1] + own_norm).astype(jnp.bfloat16), "seq", 1).astype(jnp.float32),
        )

    carried_mem, carried_norm = lax.fori_loop(
        0, lax.axis_size("seq") - 1, pass_along, (zero_mem, zero_norm)
    )
    inner_mem = jnp.concatenate([zero_mem[None], jnp.cumsum(delta_mem, axis=0)[:-1]], axis=0)
    inner_norm = jnp.concatenate([zero_norm[None], jnp.cumsum(delta_norm, axis=0)[:-1]], axis=0)
    mem_before = mem_init[None] + carried_mem[None] + inner_mem
    norm_before = norm_init[None] + carried_norm[None] + inner_norm
    query_feats = feature_map(query_seg.astype(jnp.float32))
    numer = jnp.einsum("nskgi,nkij->nskgj", query_feats, mem_before, precision=highest)
    denom = jnp.einsum("nskgi,nki->nskg", query_feats, norm_before, precision=highest)
    retrieved = numer / denom[..., None]
    score_scale = 1.0 / math.sqrt(HD)
    causal = lax.broadcasted_iota(jnp.int32, (SEG, SEG), 0) >= lax.broadcasted_iota(
        jnp.int32, (SEG, SEG), 1
    )
    scores = (
        jnp.einsum("nqkgd,nskd->nkgqs", query_seg, key_seg, preferred_element_type=jnp.float32)
        * score_scale
    )
    scores = jnp.where(causal, scores, -1e30)
    peak = jnp.max(scores, axis=-1, keepdims=True)
    expd = jnp.exp(scores - peak)
    probs = (expd / jnp.sum(expd, axis=-1, keepdims=True)).astype(jnp.bfloat16)
    local = jnp.einsum("nkgqs,nskd->nqkgd", probs, value_seg, preferred_element_type=jnp.float32)
    gate_mix = jax.nn.sigmoid(gate_bias).reshape(kv_local, group)
    mixed = (
        gate_mix[None, None, :, :, None] * retrieved
        + (1.0 - gate_mix)[None, None, :, :, None] * local
    )
    mixed = mixed.astype(jnp.bfloat16).reshape(token_count, kv_local * group * HD)
    partial_out = jnp.dot(
        mixed, lax.all_gather(wo, "seq", axis=1, tiled=True), preferred_element_type=jnp.float32
    )
    return lax.psum_scatter(
        partial_out.astype(jnp.bfloat16), "head", scatter_dimension=1, tiled=True
    )


def solution(mesh):
    placed = (
        P("seq", None),
        P(),
        P("seq", "head"),
        P("seq", "head"),
        P("seq", "head"),
        P("head", "seq"),
        P("head"),
        P("head", None, None),
        P("head", None),
    )
    return jax.shard_map(
        per_device, mesh=mesh, in_specs=placed, out_specs=P("seq", "head"), check_vma=False
    )
```

profile of v0, /device:TPU:24, one launch (start us, length us, event | category | flops | bytes accessed | tf_op | source)
XLA Modules:
  0.0 460.3 jit_solution(8971413726792928883)
XLA Ops:
  10.9 5.1 %fusion.3 = f32[1024]{0:T(1024)S(1)} fusion(bf16[1024,4096]{1,0:T(8,128)(2,1)} %param.11), kind=kLoop, calls=%fused_computation.7 | loop fusion | flops 12581888 | bytes 8392704 | tf_op jit(solution)/shard_map/reduce_sum | solution.py:28
  16.0 42.2 %all-gather.5.cloned.1.call-done = bf16[4096,256]{1,0:T(8,128)(2,1)} async-done(((bf16[512,256]{1,0:T(8,128)(2,1)}), bf16[4096,256]{1,0:T(8,128)(2,1)}) %all-gather.5.cloned.1.call-update) | async-done | bytes 2097168 | tf_op jit(solution)/shard_map/all_gather | solution.py:36
  58.3 6.4 %fusion.37 = (f32[256]{0:T(256)S(1)}, bf16[1024,256]{1,0:T(8,128)(2,1)S(1)}) fusion(bf16[4096,256]{1,0:T(8,128)(2,1)} %all-gather.5.cloned.1.call-done, bf16[1024,4096]{1,0:T(8,128)(2,1)} %param.11, f32[4096]{0:T(1024)S(1)} %copy-done.3, f32[1024]{0:T(1024)S(1)} %add_rsqrt_fusion), kind=kOutput, calls=%fused_computation.52 | convolution fusion | flops 2166095616 | bytes 11031552 | tf_op jit(solution)/shard_map/dot_general | solution.py:33
  65.5 42.7 %all-gather.7.cloned.1.call-done = bf16[4096,256]{1,0:T(8,128)(2,1)} async-done(((bf16[512,256]{1,0:T(8,128)(2,1)}), bf16[4096,256]{1,0:T(8,128)(2,1)}) %all-gather.7.cloned.1.call-update) | async-done | bytes 2097168 | tf_op jit(solution)/shard_map/all_gather | solution.py:37
  108.2 6.4 %convolution_convert_fusion.2 = bf16[1024,256]{1,0:T(8,128)(2,1)S(1)} fusion(bf16[4096,256]{1,0:T(8,128)(2,1)} %all-gather.7.cloned.1.call-done, bf16[1024,4096]{1,0:T(8,128)(2,1)} %param.11, f32[4096]{0:T(1024)S(1)} %copy-done.3, f32[1024]{0:T(1024)S(1)} %add_rsqrt_fusion), kind=kOutput, calls=%fused_computation.47 | convolution fusion | flops 2164523008 | bytes 11030528 | tf_op jit(solution)/shard_map/dot_general | solution.py:33
  116.1 67.8 %while.13 = (s32[]{:T(128)}, f32[2,128,128]{2,1,0:T(8,128)S(1)}, f32[2,128]{1,0:T(2,128)S(1)}, f32[2,128,128]{2,1,0:T(8,128)S(1)}, f32[2,128]{1,0:T(2,128)S(1)}, /*index=5*/s32[]{:T(128)}, s32[]{:T(128)}) while((s32[]{:T(128)}, f32[2,128,128]{2,1,0:T(8,128)S(1)}, f32[2,128]{1,0:T(2,128)S(1)}, f32[2,128,128]{2,1,0:T(8,128)S(1)}, ...), condition=%wide.region_4.5_spmd.clone, body=%wide.region_3.4_spmd.clone.sunk | while | flops 132099 | bytes 792744 | solution.py:63
  120.5 4.6 collective-permute-done.1
  129.1 6.2 %collective-permute-done.1 = bf16[2,128]{1,0:T(2,128)(2,1)S(1)} collective-permute-done((bf16[2,128]{1,0:T(2,128)(2,1)S(1)}, bf16[2,128]{1,0:T(2,128)(2,1)S(1)}, u32[]{:S(2)}, u32[]{:S(2)}) %collective-permute-start.1) | collective-permute-done | bytes 544 | tf_op jit(solution)/shard_map/while/body/eval_jaxpr/ppermute | solution.py:17
  139.2 6.2 %collective-permute-done.1 = bf16[2,128]{1,0:T(2,128)(2,1)S(1)} collective-permute-done((bf16[2,128]{1,0:T(2,128)(2,1)S(1)}, bf16[2,128]{1,0:T(2,128)(2,1)S(1)}, u32[]{:S(2)}, u32[]{:S(2)}) %collective-permute-start.1) | collective-permute-done | bytes 544 | tf_op jit(solution)/shard_map/while/body/eval_jaxpr/ppermute | solution.py:17
  149.4 6.6 %collective-permute-done.1 = bf16[2,128]{1,0:T(2,128)(2,1)S(1)} collective-permute-done((bf16[2,128]{1,0:T(2,128)(2,1)S(1)}, bf16[2,128]{1,0:T(2,128)(2,1)S(1)}, u32[]{:S(2)}, u32[]{:S(2)}) %collective-permute-start.1) | collective-permute-done | bytes 544 | tf_op jit(solution)/shard_map/while/body/eval_jaxpr/ppermute | solution.py:17
  160.0 4.4 collective-permute-done.1
  168.3 4.6 collective-permute-done.1
  176.8 7.1 %collective-permute-done.1 = bf16[2,128]{1,0:T(2,128)(2,1)S(1)} collective-permute-done((bf16[2,128]{1,0:T(2,128)(2,1)S(1)}, bf16[2,128]{1,0:T(2,128)(2,1)S(1)}, u32[]{:S(2)}, u32[]{:S(2)}) %collective-permute-start.1) | collective-permute-done | bytes 544 | tf_op jit(solution)/shard_map/while/body/eval_jaxpr/ppermute | solution.py:17
  184.0 57.5 %all-gather.9.cloned.1.call-done = bf16[4096,1024]{1,0:T(8,128)(2,1)} async-done(((bf16[512,1024]{1,0:T(8,128)(2,1)}), bf16[4096,1024]{1,0:T(8,128)(2,1)}) %all-gather.9.cloned.1.call-update) | async-done | bytes 8388624 | tf_op jit(solution)/shard_map/all_gather | solution.py:35
  241.5 14.7 %convolution_convert_fusion.1 = bf16[1024,1024]{1,0:T(8,128)(2,1)} fusion(bf16[4096,1024]{1,0:T(8,128)(2,1)} %all-gather.9.cloned.1.call-done, bf16[1024,4096]{1,0:T(8,128)(2,1)} %param.11, f32[4096]{0:T(1024)S(1)} %copy-done.3, f32[1024]{0:T(1024)S(1)} %add_rsqrt_fusion), kind=kOutput, calls=%fused_computation.34 | convolution fusion | flops 8607760384 | bytes 18894848 | tf_op jit(solution)/shard_map/dot_general | solution.py:33
  256.2 3.2 reshape.38
  259.4 5.4 %fusion.15 = f32[2,2,1,512,4]{2,3,4,1,0:T(8,128)} fusion(f32[2,2,128,1,1]{2,3,4,1,0:T(1,128)S(1)} %bitcast.47, bf16[2,512,2,4,128]{4,3,2,1,0:T(4,128)(2,1)S(1)} %reshape.38), kind=kOutput, calls=%fused_computation.28 | convolution fusion | flops 17825792 | bytes 2131968 | tf_op jit(solution)/shard_map/nskgi,nki->nskg/dot_general | solution.py:72
  267.9 6.6 %fusion.17 = f32[2,2,128,512,4]{3,2,4,1,0:T(8,128)} fusion(bf16[2,512,2,4,128]{4,3,2,1,0:T(4,128)(2,1)S(1)} %reshape.38, f32[1,2,128,128]{3,2,1,0:T(8,128)S(1)} %slice-done, f32[2,128,128]{2,1,0:T(8,128)S(1)} %add.80), kind=kOutput, calls=%fused_computation.29 | convolution fusion | flops 1615921152 | bytes 6553600 | tf_op jit(solution)/shard_map/nskgi,nkij->nskgj/dot_general | solution.py:71
  274.5 10.2 %fusion.66 = (f32[2,2,4,512]{3,2,1,0:T(4,128)S(1)}, f32[2,2,4,512,512]{3,4,2,1,0:T(8,128)}) fusion(pred[512,512]{0,1:T(8,128)(4,1)} %iota_compare_fusion, bf16[2,512,2,4,128]{4,3,2,1,0:T(4,128)(2,1)S(1)} %reshape.38, bf16[2,512,2,128,1]{3,2,1,0,4:T(2,128)(2,1)S(1)} %bitcast.43), kind=kOutput, calls=%fused_computation.80 | convolution fusion | flops 1090519552 | bytes 19693568 | tf_op jit(solution)/shard_map/sub | solution.py:84
  284.7 10.1 %fusion.13 = bf16[2,512,2,4,128]{1,4,3,2,0:T(8,128)(2,1)} fusion(f32[2,2,128,512,4]{3,2,4,1,0:T(8,128)} %fusion.17, f32[2,2,4,512,512]{3,4,2,1,0:T(8,128)} %get-tuple-element.68, f32[2,2,4,512]{3,2,1,0:T(4,128)S(1)} %get-tuple-element.67, f32[2,4]{1,0:T(2,128)S(1)} %broadcast_subtract_fusion, f32[2,512,2,4]{1,3,2,0:T(4,128)S(1)} %bitcast.45, ...), kind=kOutput, calls=%fused_computation.25 | convolution fusion | flops 1087373312 | bytes 23658560 | tf_op jit(solution)/shard_map/nkgqs,nskd->nqkgd/dot_general | solution.py:86
  294.8 3.1 copy.26
  300.6 66.5 %all-gather.11.cloned.1.call-done = bf16[1024,4096]{1,0:T(8,128)(2,1)} async-done(((bf16[1024,512]{1,0:T(8,128)(2,1)}), bf16[1024,4096]{1,0:T(8,128)(2,1)}) %all-gather.11.cloned.1.call-update) | async-done | bytes 8388624 | tf_op jit(solution)/shard_map/all_gather | solution.py:94
  367.1 14.7 %convolution_convert_fusion = bf16[1024,4096]{1,0:T(8,128)(2,1)} fusion(bf16[1024,1024]{1,0:T(8,128)(2,1)} %reshape.39, bf16[1024,4096]{1,0:T(8,128)(2,1)} %all-gather.11.cloned.1.call-done), kind=kOutput, calls=%fused_computation.18 | convolution fusion | flops 8594128896 | bytes 18874368 | tf_op jit(solution)/shard_map/dot_general | solution.py:93
  381.8 72.0 %reduce-scatter.2.cloned.1.call-done = bf16[1024,1024]{1,0:T(8,128)(2,1)} async-done(((bf16[1024,4096]{1,0:T(8,128)(2,1)}), bf16[1024,1024]{1,0:T(8,128)(2,1)}) %reduce-scatter.2.cloned.1.call-update) | async-done | bytes 2097168 | tf_op jit(solution)/shard_map/reduce_scatter | solution.py:96
  (89 shorter events, 40.1 us)
Async XLA Ops:
  6.5 51.7 %all-gather.5.cloned.1.call-start = ((), (), s32[]{:S(2)}) async-start(), calls=%async_computation.1 | async-start | bytes 2359296 | tf_op jit(solution)/shard_map/all_gather | solution.py:36
  7.3 100.9 %all-gather.7.cloned.1.call-start = ((), (), s32[]{:S(2)}) async-start(), calls=%async_computation.2 | async-start | bytes 2359296 | tf_op jit(solution)/shard_map/all_gather | solution.py:37
  8.0 233.5 %all-gather.9.cloned.1.call-start = ((), (), s32[]{:S(2)}) async-start(), calls=%async_computation.3 | async-start | bytes 9437184 | tf_op jit(solution)/shard_map/all_gather | solution.py:35
  8.7 358.3 %all-gather.11.cloned.1.call-start = ((), (), s32[]{:S(2)}) async-start(), calls=%async_computation.4 | async-start | bytes 9437184 | tf_op jit(solution)/shard_map/all_gather | solution.py:94
  9.3 444.5 %reduce-scatter.2.cloned.1.call-start = ((), (), s32[]{:S(2)}) async-start(), calls=%async_computation.5 | async-start | bytes 10485760 | tf_op jit(solution)/shard_map/reduce_scatter | solution.py:96
  10.9 47.3 %copy-start.3 = (f32[4096]{0:T(1024)S(1)}, f32[4096]{0:T(1024)}, u32[]{:S(2)}) copy-start(f32[4096]{0:T(1024)} %param.12) | copy-start | bytes 49156
  114.6 69.4 %copy-start.1 = (f32[2,128,128]{2,1,0:T(8,128)S(1)}, f32[2,128,128]{2,1,0:T(8,128)}, u32[]{:S(2)}) copy-start(f32[2,128,128]{2,1,0:T(8,128)} %param.18) | copy-start | bytes 393220
  114.6 69.4 %copy-start.2 = (f32[2,128]{1,0:T(2,128)S(1)}, f32[2,128]{1,0:T(2,128)}, u32[]{:S(2)}) copy-start(f32[2,128]{1,0:T(2,128)} %param.19) | copy-start | bytes 3076
  115.7 140.5 %copy-start = (f32[2,2,128,128]{3,2,1,0:T(8,128)}, f32[2,2,128,128]{3,2,1,0:T(8,128)S(1)}, u32[]{:S(2)}) copy-start(f32[2,2,128,128]{3,2,1,0:T(8,128)S(1)} %fusion.75) | copy-start | bytes 786436
  116.1 9.0 %collective-permute-start = (bf16[2,128,128]{2,1,0:T(8,128)(2,1)S(1)}, bf16[2,128,128]{2,1,0:T(8,128)(2,1)S(1)}, u32[]{:S(2)}, u32[]{:S(2)}) collective-permute-start(bf16[2,128,128]{2,1,0:T(8,128)(2,1)S(1)} %fusion.87), channel_id=1, source_target_pairs={{0,4},{4,8},{8,12},{12,16},{16,20},{20,24},{24,28},{1,5},{5,9},{9,... | collective-permute-start | bytes 196616 | tf_op jit(solution)/shard_map/while/body/eval_jaxpr/ppermute | solution.py:17
  118.6 6.5 %collective-permute-start.1 = (bf16[2,128]{1,0:T(2,128)(2,1)S(1)}, bf16[2,128]{1,0:T(2,128)(2,1)S(1)}, u32[]{:S(2)}, u32[]{:S(2)}) collective-permute-start(bf16[2,128]{1,0:T(2,128)(2,1)S(1)} %fusion.88), channel_id=1, source_target_pairs={{0,4},{4,8},{8,12},{12,16},{16,20},{20,24},{24,28},{1,5},{5,9},{9,... | collective-permute-start | bytes 1544 | tf_op jit(solution)/shard_map/while/body/eval_jaxpr/ppermute | solution.py:17
  125.2 10.1 %collective-permute-start = (bf16[2,128,128]{2,1,0:T(8,128)(2,1)S(1)}, bf16[2,128,128]{2,1,0:T(8,128)(2,1)S(1)}, u32[]{:S(2)}, u32[]{:S(2)}) collective-permute-start(bf16[2,128,128]{2,1,0:T(8,128)(2,1)S(1)} %fusion.87), channel_id=1, source_target_pairs={{0,4},{4,8},{8,12},{12,16},{16,20},{20,24},{24,28},{1,5},{5,9},{9,... | collective-permute-start | bytes 196616 | tf_op jit(solution)/shard_map/while/body/eval_jaxpr/ppermute | solution.py:17
  127.1 8.2 %collective-permute-start.1 = (bf16[2,128]{1,0:T(2,128)(2,1)S(1)}, bf16[2,128]{1,0:T(2,128)(2,1)S(1)}, u32[]{:S(2)}, u32[]{:S(2)}) collective-permute-start(bf16[2,128]{1,0:T(2,128)(2,1)S(1)} %fusion.88), channel_id=1, source_target_pairs={{0,4},{4,8},{8,12},{12,16},{16,20},{20,24},{24,28},{1,5},{5,9},{9,... | collective-permute-start | bytes 1544 | tf_op jit(solution)/shard_map/while/body/eval_jaxpr/ppermute | solution.py:17
  135.4 10.1 %collective-permute-start = (bf16[2,128,128]{2,1,0:T(8,128)(2,1)S(1)}, bf16[2,128,128]{2,1,0:T(8,128)(2,1)S(1)}, u32[]{:S(2)}, u32[]{:S(2)}) collective-permute-start(bf16[2,128,128]{2,1,0:T(8,128)(2,1)S(1)} %fusion.87), channel_id=1, source_target_pairs={{0,4},{4,8},{8,12},{12,16},{16,20},{20,24},{24,28},{1,5},{5,9},{9,... | collective-permute-start | bytes 196616 | tf_op jit(solution)/shard_map/while/body/eval_jaxpr/ppermute | solution.py:17
  137.3 8.2 %collective-permute-start.1 = (bf16[2,128]{1,0:T(2,128)(2,1)S(1)}, bf16[2,128]{1,0:T(2,128)(2,1)S(1)}, u32[]{:S(2)}, u32[]{:S(2)}) collective-permute-start(bf16[2,128]{1,0:T(2,128)(2,1)S(1)} %fusion.88), channel_id=1, source_target_pairs={{0,4},{4,8},{8,12},{12,16},{16,20},{20,24},{24,28},{1,5},{5,9},{9,... | collective-permute-start | bytes 1544 | tf_op jit(solution)/shard_map/while/body/eval_jaxpr/ppermute | solution.py:17
  145.5 10.5 %collective-permute-start = (bf16[2,128,128]{2,1,0:T(8,128)(2,1)S(1)}, bf16[2,128,128]{2,1,0:T(8,128)(2,1)S(1)}, u32[]{:S(2)}, u32[]{:S(2)}) collective-permute-start(bf16[2,128,128]{2,1,0:T(8,128)(2,1)S(1)} %fusion.87), channel_id=1, source_target_pairs={{0,4},{4,8},{8,12},{12,16},{16,20},{20,24},{24,28},{1,5},{5,9},{9,... | collective-permute-start | bytes 196616 | tf_op jit(solution)/shard_map/while/body/eval_jaxpr/ppermute | solution.py:17
  147.5 8.6 %collective-permute-start.1 = (bf16[2,128]{1,0:T(2,128)(2,1)S(1)}, bf16[2,128]{1,0:T(2,128)(2,1)S(1)}, u32[]{:S(2)}, u32[]{:S(2)}) collective-permute-start(bf16[2,128]{1,0:T(2,128)(2,1)S(1)} %fusion.88), channel_id=1, source_target_pairs={{0,4},{4,8},{8,12},{12,16},{16,20},{20,24},{24,28},{1,5},{5,9},{9,... | collective-permute-start | bytes 1544 | tf_op jit(solution)/shard_map/while/body/eval_jaxpr/ppermute | solution.py:17
  156.1 8.3 %collective-permute-start = (bf16[2,128,128]{2,1,0:T(8,128)(2,1)S(1)}, bf16[2,128,128]{2,1,0:T(8,128)(2,1)S(1)}, u32[]{:S(2)}, u32[]{:S(2)}) collective-permute-start(bf16[2,128,128]{2,1,0:T(8,128)(2,1)S(1)} %fusion.87), channel_id=1, source_target_pairs={{0,4},{4,8},{8,12},{12,16},{16,20},{20,24},{24,28},{1,5},{5,9},{9,... | collective-permute-start | bytes 196616 | tf_op jit(solution)/shard_map/while/body/eval_jaxpr/ppermute | solution.py:17
  158.0 6.3 %collective-permute-start.1 = (bf16[2,128]{1,0:T(2,128)(2,1)S(1)}, bf16[2,128]{1,0:T(2,128)(2,1)S(1)}, u32[]{:S(2)}, u32[]{:S(2)}) collective-permute-start(bf16[2,128]{1,0:T(2,128)(2,1)S(1)} %fusion.88), channel_id=1, source_target_pairs={{0,4},{4,8},{8,12},{12,16},{16,20},{20,24},{24,28},{1,5},{5,9},{9,... | collective-permute-start | bytes 1544 | tf_op jit(solution)/shard_map/while/body/eval_jaxpr/ppermute | solution.py:17
  164.4 8.4 %collective-permute-start = (bf16[2,128,128]{2,1,0:T(8,128)(2,1)S(1)}, bf16[2,128,128]{2,1,0:T(8,128)(2,1)S(1)}, u32[]{:S(2)}, u32[]{:S(2)}) collective-permute-start(bf16[2,128,128]{2,1,0:T(8,128)(2,1)S(1)} %fusion.87), channel_id=1, source_target_pairs={{0,4},{4,8},{8,12},{12,16},{16,20},{20,24},{24,28},{1,5},{5,9},{9,... | collective-permute-start | bytes 196616 | tf_op jit(solution)/shard_map/while/body/eval_jaxpr/ppermute | solution.py:17
  166.4 6.5 %collective-permute-start.1 = (bf16[2,128]{1,0:T(2,128)(2,1)S(1)}, bf16[2,128]{1,0:T(2,128)(2,1)S(1)}, u32[]{:S(2)}, u32[]{:S(2)}) collective-permute-start(bf16[2,128]{1,0:T(2,128)(2,1)S(1)} %fusion.88), channel_id=1, source_target_pairs={{0,4},{4,8},{8,12},{12,16},{16,20},{20,24},{24,28},{1,5},{5,9},{9,... | collective-permute-start | bytes 1544 | tf_op jit(solution)/shard_map/while/body/eval_jaxpr/ppermute | solution.py:17
  172.9 11.0 %collective-permute-start = (bf16[2,128,128]{2,1,0:T(8,128)(2,1)S(1)}, bf16[2,128,128]{2,1,0:T(8,128)(2,1)S(1)}, u32[]{:S(2)}, u32[]{:S(2)}) collective-permute-start(bf16[2,128,128]{2,1,0:T(8,128)(2,1)S(1)} %fusion.87), channel_id=1, source_target_pairs={{0,4},{4,8},{8,12},{12,16},{16,20},{20,24},{24,28},{1,5},{5,9},{9,... | collective-permute-start | bytes 196616 | tf_op jit(solution)/shard_map/while/body/eval_jaxpr/ppermute | solution.py:17
  174.9 9.0 %collective-permute-start.1 = (bf16[2,128]{1,0:T(2,128)(2,1)S(1)}, bf16[2,128]{1,0:T(2,128)(2,1)S(1)}, u32[]{:S(2)}, u32[]{:S(2)}) collective-permute-start(bf16[2,128]{1,0:T(2,128)(2,1)S(1)} %fusion.88), channel_id=1, source_target_pairs={{0,4},{4,8},{8,12},{12,16},{16,20},{20,24},{24,28},{1,5},{5,9},{9,... | collective-permute-start | bytes 1544 | tf_op jit(solution)/shard_map/while/body/eval_jaxpr/ppermute | solution.py:17
  259.4 8.4 %slice-start = ((f32[2,2,128,128]{3,2,1,0:T(8,128)}), f32[1,2,128,128]{3,2,1,0:T(8,128)S(1)}, s32[]{:S(2)}) async-start(f32[2,2,128,128]{3,2,1,0:T(8,128)} %copy-done), calls=%async_computation.6 | async-start | bytes 262144 | tf_op jit(solution)/shard_map/slice | solution.py:66
Sparse Core Ops, SparseCore 0:
  9.5 48.7 all-gather.4
  60.4 47.7 all-gather.6
  110.3 131.0 all-gather.8
  243.4 123.6 all-gather.10
  381.9 71.7 reduce-scatter.1
where the time goes:
time: 463 us; the launch traced here: 460 us
  waiting for transfers between devices  323 us (70%)
  matrix products  75.4 us (16%)
  starting transfers between devices  27.6 us (6%)
  between operations  13.3 us (3%)
  local copies, waits for them, and re-layouts  13.1 us (3%)
  other arithmetic  7.35 us (2%)
    reduce_scatter x1, waiting for transfers between devices, per_device(): lax.psum_scatter(partial_out.astype(jnp.bfloat16), 'head', scatter_dimens...  72 us
    all_gather x1, waiting for transfers between devices, per_device(): lax.all_gather(wo, 'seq', axis=1, tiled=True)  66.5 us
    all_gather x1, waiting for transfers between devices, per_device(): query_wide = project(lax.all_gather(wq, 'seq', axis=0, tiled=True))  57.5 us
    all_gather x1, waiting for transfers between devices, per_device(): value_wide = project(lax.all_gather(wv, 'seq', axis=0, tiled=True))  42.7 us
    all_gather x1, waiting for transfers between devices, per_device(): key_wide = project(lax.all_gather(wk, 'seq', axis=0, tiled=True))  42.2 us
    ppermute x14, waiting for transfers between devices, from_behind(): return lax.ppermute(block, axis, route)  39.7 us
    dot_general x3, matrix products, project(): return jnp.dot(normed, shard_piece, preferred_element_type=jnp.float32)  27.5 us
    ppermute x14, starting transfers between devices, from_behind(): return lax.ppermute(block, axis, route)  27.4 us
  transfers between devices with their start and end apart: 19, of which 12 were waited for; matrix products, arithmetic and copies ran while one was open for 18% of the time, Pallas kernels for 0%

commit v1 on v0

v1 whole, which is shorter than its diff:
```python
import functools
import math

import jax
import jax.numpy as jnp
from jax import lax
from jax.experimental import pallas as pl
from jax.experimental.pallas import tpu as pltpu
from jax.sharding import PartitionSpec as P

HD = 128
SEG = 512
NORM_ROWS = 16
MEM_ROWS = HD + NORM_ROWS
MESH = pl.DeviceIdType.MESH
KV, Q, WO, MEM = range(4)


def feature_map(values_in):
    return jnp.where(values_in > 0, values_in + 1.0, jnp.exp(jnp.minimum(values_in, 0.0)))


def layer_kernel(
    n,
    heads_axis,
    tokens,
    gain,
    wq,
    wk,
    wv,
    wo,
    gates,
    mem_init,
    norm_init,
    out,
    normed,
    kv_full,
    q_full,
    wo_full,
    mem_full,
    acc_kv,
    acc_q,
    keys,
    vals,
    queries,
    deltas,
    delta_norms,
    memory,
    mixed,
    got,
    xgot,
    ring_send,
    ring_recv,
    give_send,
    give_recv,
    x_send,
    x_recv,
    load_sem,
):
    me = lax.axis_index("seq")
    head = lax.axis_index("head")
    hops = n // 2
    per_head = n // heads_axis
    rows_in = wq.shape[0]
    token_count = tokens.shape[0]
    kv_width = wk.shape[1]
    q_heads = wq.shape[1] // HD
    kv_heads = kv_width // HD
    group = q_heads // kv_heads
    segments = token_count // SEG
    width = tokens.shape[1]
    block = wo.shape[1]
    tile = 256

    odd = lax.rem(me, 2)
    pos = (1 - odd) * lax.div(me, 2) + odd * (n - 1 - lax.div(me, 2))

    def seq_of(place):
        place = lax.rem(place + n, n)
        far = lax.div(place, hops)
        return (1 - far) * 2 * place + far * (2 * (n - place) - 1)

    sides = (seq_of(pos + 1), seq_of(pos - 1))
    core = lax.rem(head, 2)
    partner = head + 1 - 2 * core
    across = lax.rem(head + heads_axis // 2, heads_axis)

    loads = [
        pltpu.make_async_copy(wk, kv_full.at[me, :, pl.ds(0, kv_width)], load_sem.at[0]),
        pltpu.make_async_copy(wv, kv_full.at[me, :, pl.ds(kv_width, kv_width)], load_sem.at[1]),
        pltpu.make_async_copy(wq, q_full.at[me], load_sem.at[2]),
        pltpu.make_async_copy(wo, wo_full.at[me], load_sem.at[3]),
    ]
    for i in range(n):
        loads.append(
            pltpu.make_async_copy(
                tokens.at[:, pl.ds(i * rows_in, rows_in)], normed.at[i], load_sem.at[4 + i]
            )
        )
    for load in loads:
        load.start()

    barrier = pltpu.get_barrier_semaphore()
    for side in sides:
        pl.semaphore_signal(barrier, inc=1, device_id=(side, head), device_id_type=MESH)
    for other in (partner, across):
        pl.semaphore_signal(barrier, inc=1, device_id=(me, other), device_id_type=MESH)
    pl.semaphore_wait(barrier, 4)

    fulls = (kv_full, q_full, wo_full, mem_full)

    def ring(kind, way, hop, part):
        owner = seq_of(pos - hop + 1) if way == 0 else seq_of(pos + hop - 1)
        half = fulls[kind].shape[1] // 2
        view = fulls[kind].at[owner, pl.ds(part * half, half)]
        return pltpu.make_async_remote_copy(
            src_ref=view,
            dst_ref=view,
            send_sem=ring_send.at[kind, way, hop - 1, part],
            recv_sem=ring_recv.at[kind, way, hop - 1, part],
            device_id=(sides[way], head),
            device_id_type=MESH,
        )

    def arrival(kind, way, hop, part):
        owner = seq_of(pos - hop) if way == 0 else seq_of(pos + hop)
        half = fulls[kind].shape[1] // 2
        view = fulls[kind].at[owner, pl.ds(part * half, half)]
        return pltpu.make_async_remote_copy(
            src_ref=view,
            dst_ref=view,
            send_sem=ring_send.at[kind, way, hop - 1, part],
            recv_sem=ring_recv.at[kind, way, hop - 1, part],
            device_id=(sides[way], head),
            device_id_type=MESH,
        )

    def send_first(kind):
        for part in range(2):
            for way in range(2):
                ring(kind, way, 1, part).start()

    def forward(kind, hop):
        for step in range(2):
            for way in range(2):
                part = step if way == 0 else 1 - step
                arrival(kind, way, hop, part).wait_recv()
                if step == 0:
                    ring(kind, way, hop + 1, part).start()
                else:

                    @pl.when(hop + 1 < hops)
                    def _():
                        ring(kind, way, hop + 1, part).start()

    def take_last(kind):
        for way in range(2):
            arrival(kind, way, hops, way).wait_recv()

    loads[0].wait()
    loads[1].wait()
    send_first(KV)
    loads[2].wait()
    send_first(Q)
    loads[3].wait()
    for load in loads[4:]:
        load.wait()

    def norm_rows(i, carry):
        rows = pl.ds(pl.multiple_of(i * 64, 64), 64)
        total = jnp.zeros((64, 1), jnp.float32)
        for b in range(n):
            x = normed[b, rows, :].astype(jnp.float32)
            total = total + jnp.sum(x * x, axis=-1, keepdims=True)
        scale = lax.rsqrt(total * (1.0 / width) + 1e-05)
        for b in range(n):
            x = normed[b, rows, :].astype(jnp.float32)
            normed[b, rows, :] = (x * scale * gain[b]).astype(jnp.bfloat16)
        return carry

    lax.fori_loop(0, token_count // 64, norm_rows, 0)

    def project(acc, full, owner, first=False):
        def body(i, carry):
            rows = pl.ds(pl.multiple_of(i * tile, tile), tile)
            product = jnp.dot(
                normed[owner, rows, :], full[owner], preferred_element_type=jnp.float32
            )
            if first:
                acc[rows, :] = product
            else:
                acc[rows, :] += product
            return carry

        lax.fori_loop(0, token_count // tile, body, 0)

    def project_hop(acc, full, hop):
        def body(side, carry):
            project(acc, full, seq_of(pos - hop + 2 * hop * side))
            return carry

        lax.fori_loop(0, 2, body, 0)

    project(acc_kv, kv_full, me, True)

    def kv_step(hop, carry):
        forward(KV, hop)
        project_hop(acc_kv, kv_full, hop)
        return carry

    lax.fori_loop(1, hops, kv_step, 0)
    take_last(KV)
    forward(Q, 1)
    project(acc_kv, kv_full, seq_of(pos + hops))

    for j in range(kv_heads):
        for s in range(segments):
            rows = slice(s * SEG, (s + 1) * SEG)
            key = acc_kv[rows, j * HD : (j + 1) * HD].astype(jnp.bfloat16)
            value = acc_kv[rows, kv_width + j * HD : kv_width + (j + 1) * HD].astype(jnp.bfloat16)
            keys[j, rows, :] = key
            vals[j, rows, :] = value
            feats = feature_map(key.astype(jnp.float32))
            deltas[s, j] = jnp.dot(
                feats.T.astype(jnp.bfloat16), value, preferred_element_type=jnp.float32
            )
            delta_norms[s, j] = jnp.broadcast_to(jnp.sum(feats, axis=0, keepdims=True), (8, HD))
        own = deltas[0, j]
        own_norm = delta_norms[0, j]
        for s in range(1, segments):
            own = own + deltas[s, j]
            own_norm = own_norm + delta_norms[s, j]
        mem_full[me, j * MEM_ROWS : j * MEM_ROWS + HD, :] = own.astype(jnp.bfloat16)
        mem_full[me, j * MEM_ROWS + HD : (j + 1) * MEM_ROWS, :] = jnp.concatenate(
            [own_norm, own_norm], axis=0
        ).astype(jnp.bfloat16)
    send_first(MEM)

    project(acc_q, q_full, me, True)
    project_hop(acc_q, q_full, 1)

    def q_step(hop, carry):
        forward(Q, hop)
        forward(MEM, hop - 1)
        project_hop(acc_q, q_full, hop)
        return carry

    lax.fori_loop(2, hops, q_step, 0)
    send_first(WO)
    forward(MEM, hops - 1)
    take_last(Q)
    project(acc_q, q_full, seq_of(pos + hops))
    for h in range(q_heads):
        queries[h] = acc_q[:, h * HD : (h + 1) * HD].astype(jnp.bfloat16)

    score_scale = 1.0 / math.sqrt(HD)
    half_seg = SEG // 2

    def attend(h, carry):
        j = lax.div(h, group)
        columns = pl.ds(pl.multiple_of(h * HD, HD), HD)
        for s in range(segments):
            for t in range(2):
                start = s * SEG + t * half_seg
                seen = (t + 1) * half_seg
                scores = (
                    lax.dot_general(
                        queries[h, start : start + half_seg, :],
                        keys[j, s * SEG : s * SEG + seen, :],
                        (((1,), (1,)), ((), ())),
                        preferred_element_type=jnp.float32,
                    )
                    * score_scale
                )
                at_row = lax.broadcasted_iota(jnp.int32, (half_seg, seen), 0) + t * half_seg
                at_col = lax.broadcasted_iota(jnp.int32, (half_seg, seen), 1)
                scores = jnp.where(at_row >= at_col, scores, -1e30)
                expd = jnp.exp(scores - jnp.max(scores, axis=-1, keepdims=True))
                total = jnp.sum(expd, axis=-1, keepdims=True)
                summed = jnp.dot(
                    expd.astype(jnp.bfloat16),
                    vals[j, s * SEG : s * SEG + seen, :],
                    preferred_element_type=jnp.float32,
                )
                acc_q[start : start + half_seg, columns] = summed / total
        return carry

    lax.fori_loop(0, q_heads // 2, attend, 0)
    forward(WO, 1)
    lax.fori_loop(q_heads // 2, q_heads, attend, 0)

    take_last(MEM)
    for j in range(kv_heads):

        def add_earlier(s, carry):
            mem, norm = carry
            earlier = mem_full[s, j * MEM_ROWS : (j + 1) * MEM_ROWS, :].astype(jnp.float32)
            return mem + earlier[:HD], norm + earlier[HD : HD + 8]

        mem, norm = lax.fori_loop(
            0,
            me,
            add_earlier,
            (mem_init[j], jnp.broadcast_to(norm_init[j], (8, HD))),
        )
        for s in range(segments):
            memory[s, j, :, :HD] = mem.astype(jnp.bfloat16)
            memory[s, j, :, HD:] = jnp.broadcast_to(norm[:1], (HD, HD)).T.astype(jnp.bfloat16)
            if s + 1 < segments:
                mem = mem + deltas[s, j]
                norm = norm + delta_norms[s, j]

    def retrieve(h, carry):
        j = lax.div(h, group)
        columns = pl.ds(pl.multiple_of(h * HD, HD), HD)
        gate = gates[h]
        for s in range(segments):
            rows = slice(s * SEG, (s + 1) * SEG)
            feats = feature_map(queries[h, rows, :].astype(jnp.float32)).astype(jnp.bfloat16)
            both = jnp.dot(feats, memory[s, j], preferred_element_type=jnp.float32)
            retrieved = both[:, :HD] / both[:, HD:]
            mixed[rows, columns] = (
                gate * retrieved + (1.0 - gate) * acc_q[rows, columns]
            ).astype(jnp.bfloat16)
        return carry

    lax.fori_loop(0, q_heads, retrieve, 0)

    def place_of(c):
        target = lax.div(c, per_head)
        slot = lax.div(target, 2) * per_head + lax.rem(c, per_head)
        return target, slot

    def give(c):
        target, slot = place_of(c)
        return pltpu.make_async_remote_copy(
            src_ref=normed.at[c],
            dst_ref=got.at[slot],
            send_sem=give_send.at[slot],
            recv_sem=give_recv.at[slot],
            device_id=(me, partner),
            device_id_type=MESH,
        )

    def cross(c):
        return pltpu.make_async_remote_copy(
            src_ref=normed.at[c],
            dst_ref=xgot.at[lax.rem(c, per_head)],
            send_sem=x_send.at[lax.rem(c, per_head)],
            recv_sem=x_recv.at[lax.rem(c, per_head)],
            device_id=(me, across),
            device_id_type=MESH,
        )

    def emit(c):
        def body(i, carry):
            rows = pl.ds(pl.multiple_of(i * tile, tile), tile)
            normed[c, rows, :] = jnp.dot(
                mixed[rows, :], wo_full[c], preferred_element_type=jnp.float32
            ).astype(jnp.bfloat16)
            return carry

        lax.fori_loop(0, token_count // tile, body, 0)
        target, slot = place_of(c)

        @pl.when(lax.rem(target, 2) != core)
        def _():
            give(c).start()

    def finish(c):
        target, slot = place_of(c)

        @pl.when(lax.rem(target, 2) == core)
        def _():
            give(c).wait_recv()

            def body(i, carry):
                rows = pl.ds(pl.multiple_of(i * tile, tile), tile)
                normed[c, rows, :] = (
                    normed[c, rows, :].astype(jnp.float32) + got[slot, rows, :].astype(jnp.float32)
                ).astype(jnp.bfloat16)
                return carry

            @pl.when(target != head)
            def _():
                lax.fori_loop(0, token_count // tile, body, 0)
                cross(c).start()

    emit(me)
    finish(me)

    def out_step(hop, carry):
        def emit_side(side, inner):
            emit(seq_of(pos - hop + 2 * hop * side))
            return inner

        def finish_side(side, inner):
            finish(seq_of(pos - hop + 2 * hop * side))
            return inner

        lax.fori_loop(0, 2, emit_side, 0)
        lax.fori_loop(0, 2, finish_side, 0)

        @pl.when(hop + 1 < hops)
        def _():
            forward(WO, hop + 1)

        return carry

    lax.fori_loop(1, hops, out_step, 0)
    take_last(WO)
    emit(seq_of(pos + hops))
    finish(seq_of(pos + hops))

    for o in range(per_head):
        c = head * per_head + o
        cross(c).wait_recv()
        slot = lax.div(head, 2) * per_head + o

        def body(i, carry):
            rows = pl.ds(pl.multiple_of(i * tile, tile), tile)
            out[rows, o * block : (o + 1) * block] = (
                normed[c, rows, :].astype(jnp.float32)
                + got[slot, rows, :].astype(jnp.float32)
                + xgot[o, rows, :].astype(jnp.float32)
            ).astype(jnp.bfloat16)
            return carry

        lax.fori_loop(0, token_count // tile, body, 0)

    for kind in range(4):

        def drain(hop, carry):
            for way in range(2):
                for part in range(2):
                    ring(kind, way, hop, part).wait_send()
            return carry

        lax.fori_loop(1, hops, drain, 0)
        for way in range(2):
            ring(kind, way, hops, way).wait_send()

    def drain_out(c, carry):
        target, slot = place_of(c)

        @pl.when(lax.rem(target, 2) != core)
        def _():
            give(c).wait_send()

        @pl.when((lax.rem(target, 2) == core) & (target != head))
        def _():
            cross(c).wait_send()

        return carry

    lax.fori_loop(0, n, drain_out, 0)


def per_device(n, heads_axis, tokens, norm_gain, wq, wk, wv, wo, gate_bias, mem_init, norm_init):
    token_count, width = tokens.shape
    rows_in = wq.shape[0]
    q_width = wq.shape[1]
    kv_width = wk.shape[1]
    q_heads = q_width // HD
    kv_heads = kv_width // HD
    block = wo.shape[1]
    segments = token_count // SEG
    hops = n // 2
    per_head = n // heads_axis
    gates = jnp.broadcast_to(jax.nn.sigmoid(gate_bias)[:, None, None], (q_heads, 1, HD))
    gain = norm_gain.reshape(n, 1, rows_in)
    anywhere = pl.BlockSpec(memory_space=pl.ANY)
    near = pl.BlockSpec(memory_space=pltpu.VMEM)
    bf16, f32 = jnp.bfloat16, jnp.float32
    flops = 2 * token_count * (width * (q_width + 2 * kv_width) + q_width * width)
    return pl.pallas_call(
        functools.partial(layer_kernel, n, heads_axis),
        out_shape=jax.ShapeDtypeStruct((token_count, per_head * block), bf16),
        in_specs=[anywhere, near, anywhere, anywhere, anywhere, anywhere, near, near, near],
        out_specs=near,
        scratch_shapes=[
            pltpu.VMEM((n, token_count, rows_in), bf16),
            pltpu.VMEM((n, rows_in, 2 * kv_width), bf16),
            pltpu.VMEM((n, rows_in, q_width), bf16),
            pltpu.VMEM((n, q_width, block), bf16),
            pltpu.VMEM((n, kv_heads * MEM_ROWS, HD), bf16),
            pltpu.VMEM((token_count, 2 * kv_width), f32),
            pltpu.VMEM((token_count, q_width), f32),
            pltpu.VMEM((kv_heads, token_count, HD), bf16),
            pltpu.VMEM((kv_heads, token_count, HD), bf16),
            pltpu.VMEM((q_heads, token_count, HD), bf16),
            pltpu.VMEM((segments, kv_heads, HD, HD), f32),
            pltpu.VMEM((segments, kv_heads, 8, HD), f32),
            pltpu.VMEM((segments, kv_heads, HD, 2 * HD), bf16),
            pltpu.VMEM((token_count, q_width), bf16),
            pltpu.VMEM((n // 2, token_count, block), bf16),
            pltpu.VMEM((per_head, token_count, block), bf16),
            pltpu.SemaphoreType.DMA((4, 2, hops, 2)),
            pltpu.SemaphoreType.DMA((4, 2, hops, 2)),
            pltpu.SemaphoreType.DMA((n // 2,)),
            pltpu.SemaphoreType.DMA((n // 2,)),
            pltpu.SemaphoreType.DMA((per_head,)),
            pltpu.SemaphoreType.DMA((per_head,)),
            pltpu.SemaphoreType.DMA((4 + n,)),
        ],
        compiler_params=pltpu.CompilerParams(
            collective_id=0, has_side_effects=True, vmem_limit_bytes=60 * 1024 * 1024
        ),
        cost_estimate=pl.CostEstimate(
            flops=flops, bytes_accessed=2 * token_count * width, transcendentals=0
        ),
    )(tokens, gain, wq, wk, wv, wo, gates, mem_init, norm_init.reshape(kv_heads, 1, HD))


def solution(mesh):
    placed = (
        P("seq", None),
        P(),
        P("seq", "head"),
        P("seq", "head"),
        P("seq", "head"),
        P("head", "seq"),
        P("head"),
        P("head", None, None),
        P("head", None),
    )
    return jax.shard_map(
        functools.partial(per_device, mesh.shape["seq"], mesh.shape["head"]),
        mesh=mesh,
        in_specs=placed,
        out_specs=P("seq", "head"),
        check_vma=False,
    )
```

time: 463 us -> 248 us (0.54)
  waiting for transfers between devices: 323 us -> 0 us
  Pallas kernels: 0 us -> 243 us
  matrix products: 75.4 us -> 0 us
  starting transfers between devices: 27.6 us -> 0 us
  between operations: 13.3 us -> 0.01 us
  local copies, waits for them, and re-layouts: 13.1 us -> 3.76 us
  other arithmetic: 7.35 us -> 0.66 us
    pallas_call x0 -> x1, Pallas kernels: none -> 243 us  [per_device(): pl.pallas_call(functools.partial(layer_kernel, n, heads_axis), out_shape=...]
    all_gather x4 -> x0, waiting for transfers between devices: 209 us -> none  [the longest x1 66.5 us: per_device(): lax.all_gather(wo, 'seq', axis=1, tiled=True)]
    reduce_scatter x1 -> x0, waiting for transfers between devices: 72 us -> none  [per_device(): lax.psum_scatter(partial_out.astype(jnp.bfloat16), 'head', scatter_dimens...]
    dot_general x8 -> x0, matrix products: 65.2 us -> none  [the longest x3 27.5 us: project(): return jnp.dot(normed, shard_piece, preferred_element_type=jnp.float32)]
    ppermute x14 -> x0, waiting for transfers between devices: 39.7 us -> none  [from_behind(): return lax.ppermute(block, axis, route)]
    ppermute x14 -> x0, starting transfers between devices: 27.4 us -> none  [from_behind(): return lax.ppermute(block, axis, route)]
    sub x1 -> x0, matrix products: 10.2 us -> none  [per_device(): expd = jnp.exp(scores - peak)]
    reshape x5 -> x0, local copies, waits for them, and re-layouts: 6.79 us -> none  [the longest x1 3.23 us: per_device(): query_seg = queries.reshape(segments, SEG, kv_local, group, HD)]
  transfers between devices with their start and end apart: 19 -> 0, of which waited for: 12 -> 0; matrix products, arithmetic and copies ran while one was open for 18% -> 0% of each run, Pallas kernels for 0% -> 0%
where the time goes in v1:
time: 248 us
  Pallas kernels  243 us (98%)
  local copies, waits for them, and re-layouts  3.76 us (2%)
    pallas_call x1, Pallas kernels, per_device(): pl.pallas_call(functools.partial(layer_kernel, n, heads_axis), out_shape=...  243 us

profile of v1, /device:TPU:24, one launch (start us, length us, event | category | flops | bytes accessed | tf_op | source)
XLA Modules:
  0.0 247.5 jit_solution(3916534981383250454)
XLA Ops:
  0.0 0.7 add_divide_fusion
  0.7 0.7 broadcast_in_dim.2.gates
  1.3 243.1 %shard_map.91 = bf16[1024,1024]{1,0:T(8,128)(2,1)} custom-call(bf16[1024,4096]{1,0:T(8,128)(2,1)} %tokens.1, f32[8,1,512]{2,1,0:T(1,128)} %bitcast.2, bf16[512,1024]{1,0:T(8,128)(2,1)} %wq.1, bf16[512,256]{1,0:T(8,128)(2,1)} %wk.1, bf16[512,256]{1,0:T(8,128)(2,1)} %wv.1, bf16[1024,512]{1,0:T(8,128)(2,1)} %wo.1, f32[8,1,128]{2,1,0:T(1,128)} %broadcast_in_dim.2.gates, ...), custom_call_target="tpu_custom_call" | custom-call | flops 21474836480 | bytes 8388608 | tf_op jit(solution)/shard_map/pallas_call | solution.py:476
  244.5 3.1 %copy.11 = bf16[1024,1024]{1,0:T(8,128)(2,1)} copy(bf16[1024,1024]{1,0:T(8,128)(2,1)} %shard_map.91) | data formatting | bytes 4194304

commit v2 on v1

--- a/solution.py
+++ b/solution.py
@@ -13,7 +13,7 @@
 NORM_ROWS = 16
 MEM_ROWS = HD + NORM_ROWS
 MESH = pl.DeviceIdType.MESH
-KV, Q, WO, MEM = range(4)
+LOG2E = math.log2(math.e)
 
 
 def feature_map(values_in):
@@ -23,6 +23,7 @@
 def layer_kernel(
     n,
     heads_axis,
+    wo_parts,
     tokens,
     gain,
     wq,
@@ -64,13 +65,19 @@
     rows_in = wq.shape[0]
     token_count = tokens.shape[0]
     kv_width = wk.shape[1]
-    q_heads = wq.shape[1] // HD
+    q_width = wq.shape[1]
+    q_part = q_width // 2
+    q_heads = q_width // HD
     kv_heads = kv_width // HD
     group = q_heads // kv_heads
     segments = token_count // SEG
     width = tokens.shape[1]
     block = wo.shape[1]
+    sub = block // wo_parts
     tile = 256
+    kv_kind, q_kinds = 0, (1, 2)
+    wo_kinds = tuple(range(3, 3 + wo_parts))
+    mem_kind = 3 + wo_parts
 
     odd = lax.rem(me, 2)
     pos = (1 - odd) * lax.div(me, 2) + odd * (n - 1 - lax.div(me, 2))
@@ -88,13 +95,24 @@
     loads = [
         pltpu.make_async_copy(wk, kv_full.at[me, :, pl.ds(0, kv_width)], load_sem.at[0]),
         pltpu.make_async_copy(wv, kv_full.at[me, :, pl.ds(kv_width, kv_width)], load_sem.at[1]),
-        pltpu.make_async_copy(wq, q_full.at[me], load_sem.at[2]),
-        pltpu.make_async_copy(wo, wo_full.at[me], load_sem.at[3]),
     ]
+    for part in range(2):
+        loads.append(
+            pltpu.make_async_copy(
+                wq.at[:, pl.ds(part * q_part, q_part)], q_full.at[part, me], load_sem.at[2 + part]
+            )
+        )
+    for part in range(wo_parts):
+        loads.append(
+            pltpu.make_async_copy(
+                wo.at[:, pl.ds(part * sub, sub)], wo_full.at[part, me], load_sem.at[4 + part]
+            )
+        )
+    weight_loads = len(loads)
     for i in range(n):
         loads.append(
             pltpu.make_async_copy(
-                tokens.at[:, pl.ds(i * rows_in, rows_in)], normed.at[i], load_sem.at[4 + i]
+                tokens.at[:, pl.ds(i * rows_in, rows_in)], normed.at[i], load_sem.at[weight_loads + i]
             )
         )
     for load in loads:
@@ -107,7 +125,9 @@
         pl.semaphore_signal(barrier, inc=1, device_id=(me, other), device_id_type=MESH)
     pl.semaphore_wait(barrier, 4)
 
-    fulls = (kv_full, q_full, wo_full, mem_full)
+    fulls = [kv_full, q_full.at[0], q_full.at[1]]
+    fulls += [wo_full.at[part] for part in range(wo_parts)]
+    fulls.append(mem_full)
 
     def ring(kind, way, hop, part):
         owner = seq_of(pos - hop + 1) if way == 0 else seq_of(pos + hop - 1)
@@ -159,11 +179,10 @@
 
     loads[0].wait()
     loads[1].wait()
-    send_first(KV)
+    send_first(kv_kind)
     loads[2].wait()
-    send_first(Q)
-    loads[3].wait()
-    for load in loads[4:]:
+    send_first(q_kinds[0])
+    for load in loads[3:]:
         load.wait()
 
     def norm_rows(i, carry):
@@ -180,38 +199,52 @@
 
     lax.fori_loop(0, token_count // 64, norm_rows, 0)
 
-    def project(acc, full, owner, first=False):
+    def project(acc, columns, kind, owner, first=False):
         def body(i, carry):
             rows = pl.ds(pl.multiple_of(i * tile, tile), tile)
             product = jnp.dot(
-                normed[owner, rows, :], full[owner], preferred_element_type=jnp.float32
+                normed[owner, rows, :], fulls[kind][owner], preferred_element_type=jnp.float32
             )
             if first:
-                acc[rows, :] = product
+                acc[rows, columns] = product
             else:
-                acc[rows, :] += product
+                acc[rows, columns] += product
             return carry
 
         lax.fori_loop(0, token_count // tile, body, 0)
 
-    def project_hop(acc, full, hop):
+    def project_hop(acc, columns, kind, hop):
         def body(side, carry):
-            project(acc, full, seq_of(pos - hop + 2 * hop * side))
+            project(acc, columns, kind, seq_of(pos - hop + 2 * hop * side))
             return carry
 
         lax.fori_loop(0, 2, body, 0)
 
-    project(acc_kv, kv_full, me, True)
-
-    def kv_step(hop, carry):
-        forward(KV, hop)
-        project_hop(acc_kv, kv_full, hop)
-        return carry
-
-    lax.fori_loop(1, hops, kv_step, 0)
-    take_last(KV)
-    forward(Q, 1)
-    project(acc_kv, kv_full, seq_of(pos + hops))
+    kv_columns = slice(0, 2 * kv_width)
+    q_columns = [slice(part * q_part, (part + 1) * q_part) for part in range(2)]
+
+    def middle(acc, columns, kind):
+        def step(hop, carry):
+            forward(kind, hop)
+            project_hop(acc, columns, kind, hop - 1)
+            return carry
+
+        lax.fori_loop(3, hops, step, 0)
+
+    project(acc_kv, kv_columns, kv_kind, me, True)
+    forward(kv_kind, 1)
+    project_hop(acc_kv, kv_columns, kv_kind, 1)
+    forward(kv_kind, 2)
+    middle(acc_kv, kv_columns, kv_kind)
+    forward(q_kinds[0], 1)
+    project_hop(acc_kv, kv_columns, kv_kind, hops - 1)
+    take_last(kv_kind)
+    project(acc_kv, kv_columns, kv_kind, seq_of(pos + hops))
+
+    project(acc_q, q_columns[0], q_kinds[0], me, True)
+    forward(q_kinds[0], 2)
+    send_first(q_kinds[1])
+    project_hop(acc_q, q_columns[0], q_kinds[0], 1)
 
     for j in range(kv_heads):
         for s in range(segments):
@@ -234,62 +267,98 @@
         mem_full[me, j * MEM_ROWS + HD : (j + 1) * MEM_ROWS, :] = jnp.concatenate(
             [own_norm, own_norm], axis=0
         ).astype(jnp.bfloat16)
-    send_first(MEM)
-
-    project(acc_q, q_full, me, True)
-    project_hop(acc_q, q_full, 1)
-
-    def q_step(hop, carry):
-        forward(Q, hop)
-        forward(MEM, hop - 1)
-        project_hop(acc_q, q_full, hop)
-        return carry
-
-    lax.fori_loop(2, hops, q_step, 0)
-    send_first(WO)
-    forward(MEM, hops - 1)
-    take_last(Q)
-    project(acc_q, q_full, seq_of(pos + hops))
-    for h in range(q_heads):
-        queries[h] = acc_q[:, h * HD : (h + 1) * HD].astype(jnp.bfloat16)
-
-    score_scale = 1.0 / math.sqrt(HD)
+    send_first(mem_kind)
+
+    middle(acc_q, q_columns[0], q_kinds[0])
+    forward(q_kinds[1], 1)
+    project_hop(acc_q, q_columns[0], q_kinds[0], hops - 1)
+    take_last(q_kinds[0])
+    project(acc_q, q_columns[0], q_kinds[0], seq_of(pos + hops))
+
+    def round_queries(part):
+        for h in range(part * (q_heads // 2), (part + 1) * (q_heads // 2)):
+            queries[h] = acc_q[:, h * HD : (h + 1) * HD].astype(jnp.bfloat16)
+
+    exponent_scale = LOG2E / math.sqrt(HD)
     half_seg = SEG // 2
+
+    def scores_of(left, right):
+        return lax.dot_general(
+            left, right, (((1,), (1,)), ((), ())), preferred_element_type=jnp.float32
+        )
 
     def attend(h, carry):
         j = lax.div(h, group)
         columns = pl.ds(pl.multiple_of(h * HD, HD), HD)
+        at_row = lax.broadcasted_iota(jnp.int32, (half_seg, half_seg), 0)
+        at_col = lax.broadcasted_iota(jnp.int32, (half_seg, half_seg), 1)
+        allowed = at_row >= at_col
         for s in range(segments):
             for t in range(2):
                 start = s * SEG + t * half_seg
-                seen = (t + 1) * half_seg
-                scores = (
-                    lax.dot_general(
-                        queries[h, start : start + half_seg, :],
-                        keys[j, s * SEG : s * SEG + seen, :],
-                        (((1,), (1,)), ((), ())),
-                        preferred_element_type=jnp.float32,
-                    )
-                    * score_scale
-                )
-                at_row = lax.broadcasted_iota(jnp.int32, (half_seg, seen), 0) + t * half_seg
-                at_col = lax.broadcasted_iota(jnp.int32, (half_seg, seen), 1)
-                scores = jnp.where(at_row >= at_col, scores, -1e30)
-                expd = jnp.exp(scores - jnp.max(scores, axis=-1, keepdims=True))
+                query = queries[h, start : start + half_seg, :]
+                near_keys = keys[j, start : start + half_seg, :]
+                diagonal = jnp.where(allowed, scores_of(query, near_keys), -1e30)
+                peak = jnp.max(diagonal, axis=-1, keepdims=True)
+                if t:
+                    full = scores_of(query, keys[j, start - half_seg : start, :])
+                    peak = jnp.maximum(peak, jnp.max(full, axis=-1, keepdims=True))
+                expd = jnp.exp2((diagonal - peak) * exponent_scale)
                 total = jnp.sum(expd, axis=-1, keepdims=True)
                 summed = jnp.dot(
                     expd.astype(jnp.bfloat16),
-                    vals[j, s * SEG : s * SEG + seen, :],
+                    vals[j, start : start + half_seg, :],
                     preferred_element_type=jnp.float32,
                 )
+                if t:
+                    expd = jnp.exp2((full - peak) * exponent_scale)
+                    total = total + jnp.sum(expd, axis=-1, keepdims=True)
+                    summed = summed + jnp.dot(
+                        expd.astype(jnp.bfloat16),
+                        vals[j, start - half_seg : start, :],
+                        preferred_element_type=jnp.float32,
+                    )
                 acc_q[start : start + half_seg, columns] = summed / total
         return carry
 
-    lax.fori_loop(0, q_heads // 2, attend, 0)
-    forward(WO, 1)
-    lax.fori_loop(q_heads // 2, q_heads, attend, 0)
-
-    take_last(MEM)
+    half_heads = q_heads // 2
+    round_queries(0)
+    forward(q_kinds[1], 2)
+    send_first(wo_kinds[0])
+    forward(mem_kind, 1)
+    project(acc_q, q_columns[1], q_kinds[1], me, True)
+    project_hop(acc_q, q_columns[1], q_kinds[1], 1)
+    lax.fori_loop(0, half_heads // 2, attend, 0)
+
+    def q_step(hop, carry):
+        forward(q_kinds[1], hop)
+        forward(mem_kind, hop - 1)
+        project_hop(acc_q, q_columns[1], q_kinds[1], hop - 1)
+        return carry
+
+    lax.fori_loop(3, hops, q_step, 0)
+    lax.fori_loop(half_heads // 2, half_heads, attend, 0)
+    forward(wo_kinds[0], 1)
+    forward(mem_kind, hops - 1)
+    project_hop(acc_q, q_columns[1], q_kinds[1], hops - 1)
+    take_last(q_kinds[1])
+    project(acc_q, q_columns[1], q_kinds[1], seq_of(pos + hops))
+    round_queries(1)
+    forward(wo_kinds[0], 2)
+    if wo_parts > 1:
+        send_first(wo_kinds[1])
+    lax.fori_loop(half_heads, q_heads, attend, 0)
+
+    def pass_on(kind):
+        def step(hop, carry):
+            forward(kind, hop)
+            return carry
+
+        lax.fori_loop(3, hops, step, 0)
+
+    pass_on(wo_kinds[0])
+
+    take_last(mem_kind)
     for j in range(kv_heads):
 
         def add_earlier(s, carry):
@@ -313,7 +382,7 @@
     def retrieve(h, carry):
         j = lax.div(h, group)
         columns = pl.ds(pl.multiple_of(h * HD, HD), HD)
-        gate = gates[h]
+        gate = 1.0 / (1.0 + jnp.exp(-jnp.full((1, HD), gates[h], jnp.float32)))
         for s in range(segments):
             rows = slice(s * SEG, (s + 1) * SEG)
             feats = feature_map(queries[h, rows, :].astype(jnp.float32)).astype(jnp.bfloat16)
@@ -331,32 +400,35 @@
         slot = lax.div(target, 2) * per_head + lax.rem(c, per_head)
         return target, slot
 
-    def give(c):
+    def give(part, c):
         target, slot = place_of(c)
         return pltpu.make_async_remote_copy(
-            src_ref=normed.at[c],
-            dst_ref=got.at[slot],
-            send_sem=give_send.at[slot],
-            recv_sem=give_recv.at[slot],
+            src_ref=normed.at[c, :, pl.ds(part * sub, sub)],
+            dst_ref=got.at[part, slot],
+            send_sem=give_send.at[part, slot],
+            recv_sem=give_recv.at[part, slot],
             device_id=(me, partner),
             device_id_type=MESH,
         )
 
-    def cross(c):
+    def cross(part, c):
+        index = lax.rem(c, per_head)
         return pltpu.make_async_remote_copy(
-            src_ref=normed.at[c],
-            dst_ref=xgot.at[lax.rem(c, per_head)],
-            send_sem=x_send.at[lax.rem(c, per_head)],
-            recv_sem=x_recv.at[lax.rem(c, per_head)],
+            src_ref=normed.at[c, :, pl.ds(part * sub, sub)],
+            dst_ref=xgot.at[part, index],
+            send_sem=x_send.at[part, index],
+            recv_sem=x_recv.at[part, index],
             device_id=(me, across),
             device_id_type=MESH,
         )
 
-    def emit(c):
+    def emit(part, c):
+        columns = slice(part * sub, (part + 1) * sub)
+
         def body(i, carry):
             rows = pl.ds(pl.multiple_of(i * tile, tile), tile)
-            normed[c, rows, :] = jnp.dot(
-                mixed[rows, :], wo_full[c], preferred_element_type=jnp.float32
+            normed[c, rows, columns] = jnp.dot(
+                mixed[rows, :], wo_full[part, c], preferred_element_type=jnp.float32
             ).astype(jnp.bfloat16)
             return carry
 
@@ -365,70 +437,86 @@
 
         @pl.when(lax.rem(target, 2) != core)
         def _():
-            give(c).start()
-
-    def finish(c):
+            give(part, c).start()
+
+    def finish(part, c):
         target, slot = place_of(c)
+        columns = slice(part * sub, (part + 1) * sub)
 
         @pl.when(lax.rem(target, 2) == core)
         def _():
-            give(c).wait_recv()
+            give(part, c).wait_recv()
 
             def body(i, carry):
                 rows = pl.ds(pl.multiple_of(i * tile, tile), tile)
-                normed[c, rows, :] = (
-                    normed[c, rows, :].astype(jnp.float32) + got[slot, rows, :].astype(jnp.float32)
+                normed[c, rows, columns] = (
+                    normed[c, rows, columns].astype(jnp.float32)
+                    + got[part, slot, rows, :].astype(jnp.float32)
                 ).astype(jnp.bfloat16)
                 return carry
 
             @pl.when(target != head)
             def _():
                 lax.fori_loop(0, token_count // tile, body, 0)
-                cross(c).start()
-
-    emit(me)
-    finish(me)
-
-    def out_step(hop, carry):
-        def emit_side(side, inner):
-            emit(seq_of(pos - hop + 2 * hop * side))
-            return inner
-
-        def finish_side(side, inner):
-            finish(seq_of(pos - hop + 2 * hop * side))
-            return inner
-
-        lax.fori_loop(0, 2, emit_side, 0)
-        lax.fori_loop(0, 2, finish_side, 0)
-
-        @pl.when(hop + 1 < hops)
-        def _():
-            forward(WO, hop + 1)
-
-        return carry
-
-    lax.fori_loop(1, hops, out_step, 0)
-    take_last(WO)
-    emit(seq_of(pos + hops))
-    finish(seq_of(pos + hops))
-
-    for o in range(per_head):
-        c = head * per_head + o
-        cross(c).wait_recv()
-        slot = lax.div(head, 2) * per_head + o
-
-        def body(i, carry):
-            rows = pl.ds(pl.multiple_of(i * tile, tile), tile)
-            out[rows, o * block : (o + 1) * block] = (
-                normed[c, rows, :].astype(jnp.float32)
-                + got[slot, rows, :].astype(jnp.float32)
-                + xgot[o, rows, :].astype(jnp.float32)
-            ).astype(jnp.bfloat16)
+                cross(part, c).start()
+
+    def out_hops(part, first, last):
+        def out_step(hop, carry):
+            def emit_side(side, inner):
+                emit(part, seq_of(pos - hop + 2 * hop * side))
+                return inner
+
+            def finish_side(side, inner):
+                finish(part, seq_of(pos - hop + 2 * hop * side))
+                return inner
+
+            lax.fori_loop(0, 2, emit_side, 0)
+            lax.fori_loop(0, 2, finish_side, 0)
             return carry
 
-        lax.fori_loop(0, token_count // tile, body, 0)
-
-    for kind in range(4):
+        lax.fori_loop(first, last + 1, out_step, 0)
+
+    def out_one(part, c):
+        emit(part, c)
+        finish(part, c)
+
+    def collect(part):
+        for o in range(per_head):
+            c = head * per_head + o
+            cross(part, c).wait_recv()
+            slot = lax.div(head, 2) * per_head + o
+            columns = slice(part * sub, (part + 1) * sub)
+            placed = slice(o * block + part * sub, o * block + (part + 1) * sub)
+
+            def body(i, carry):
+                rows = pl.ds(pl.multiple_of(i * tile, tile), tile)
+                out[rows, placed] = (
+                    normed[c, rows, columns].astype(jnp.float32)
+                    + got[part, slot, rows, :].astype(jnp.float32)
+                    + xgot[part, o, rows, :].astype(jnp.float32)
+                ).astype(jnp.bfloat16)
+                return carry
+
+            lax.fori_loop(0, token_count // tile, body, 0)
+
+    for part in range(wo_parts):
+        kind = wo_kinds[part]
+        more = part + 1 < wo_parts
+        if more:
+            forward(wo_kinds[part + 1], 1)
+        out_one(part, me)
+        out_hops(part, 1, hops - 2)
+        if more:
+            forward(wo_kinds[part + 1], 2)
+        out_hops(part, hops - 1, hops - 1)
+        take_last(kind)
+        out_one(part, seq_of(pos + hops))
+        if more:
+            pass_on(wo_kinds[part + 1])
+    for part in range(wo_parts):
+        collect(part)
+
+    for kind in range(len(fulls)):
 
         def drain(hop, carry):
             for way in range(2):
@@ -442,14 +530,15 @@
 
     def drain_out(c, carry):
         target, slot = place_of(c)
-
-        @pl.when(lax.rem(target, 2) != core)
-        def _():
-            give(c).wait_send()
-
-        @pl.when((lax.rem(target, 2) == core) & (target != head))
-        def _():
-            cross(c).wait_send()
+        for part in range(wo_parts):
+
+            @pl.when(lax.rem(target, 2) != core)
+            def _():
+                give(part, c).wait_send()
+
+            @pl.when((lax.rem(target, 2) == core) & (target != head))
+            def _():
+                cross(part, c).wait_send()
 
         return carry
 
@@ -467,22 +556,24 @@
     segments = token_count // SEG
     hops = n // 2
     per_head = n // heads_axis
-    gates = jnp.broadcast_to(jax.nn.sigmoid(gate_bias)[:, None, None], (q_heads, 1, HD))
+    wo_parts = 2 if block % (2 * HD) == 0 else 1
+    kinds = 4 + wo_parts
     gain = norm_gain.reshape(n, 1, rows_in)
     anywhere = pl.BlockSpec(memory_space=pl.ANY)
     near = pl.BlockSpec(memory_space=pltpu.VMEM)
+    scalars = pl.BlockSpec(memory_space=pltpu.SMEM)
     bf16, f32 = jnp.bfloat16, jnp.float32
     flops = 2 * token_count * (width * (q_width + 2 * kv_width) + q_width * width)
     return pl.pallas_call(
-        functools.partial(layer_kernel, n, heads_axis),
+        functools.partial(layer_kernel, n, heads_axis, wo_parts),
         out_shape=jax.ShapeDtypeStruct((token_count, per_head * block), bf16),
-        in_specs=[anywhere, near, anywhere, anywhere, anywhere, anywhere, near, near, near],
+        in_specs=[anywhere, near, anywhere, anywhere, anywhere, anywhere, scalars, near, near],
         out_specs=near,
         scratch_shapes=[
             pltpu.VMEM((n, token_count, rows_in), bf16),
             pltpu.VMEM((n, rows_in, 2 * kv_width), bf16),
-            pltpu.VMEM((n, rows_in, q_width), bf16),
-            pltpu.VMEM((n, q_width, block), bf16),
+            pltpu.VMEM((2, n, rows_in, q_width // 2), bf16),
+            pltpu.VMEM((wo_parts, n, q_width, block // wo_parts), bf16),
             pltpu.VMEM((n, kv_heads * MEM_ROWS, HD), bf16),
             pltpu.VMEM((token_count, 2 * kv_width), f32),
             pltpu.VMEM((token_count, q_width), f32),
@@ -493,15 +584,15 @@
             pltpu.VMEM((segments, kv_heads, 8, HD), f32),
             pltpu.VMEM((segments, kv_heads, HD, 2 * HD), bf16),
             pltpu.VMEM((token_count, q_width), bf16),
-            pltpu.VMEM((n // 2, token_count, block), bf16),
-            pltpu.VMEM((per_head, token_count, block), bf16),
-            pltpu.SemaphoreType.DMA((4, 2, hops, 2)),
-            pltpu.SemaphoreType.DMA((4, 2, hops, 2)),
-            pltpu.SemaphoreType.DMA((n // 2,)),
-            pltpu.SemaphoreType.DMA((n // 2,)),
-            pltpu.SemaphoreType.DMA((per_head,)),
-            pltpu.SemaphoreType.DMA((per_head,)),
-            pltpu.SemaphoreType.DMA((4 + n,)),
+            pltpu.VMEM((wo_parts, n // 2, token_count, block // wo_parts), bf16),
+            pltpu.VMEM((wo_parts, per_head, token_count, block // wo_parts), bf16),
+            pltpu.SemaphoreType.DMA((kinds, 2, hops, 2)),
+            pltpu.SemaphoreType.DMA((kinds, 2, hops, 2)),
+            pltpu.SemaphoreType.DMA((wo_parts, n // 2)),
+            pltpu.SemaphoreType.DMA((wo_parts, n // 2)),
+            pltpu.SemaphoreType.DMA((wo_parts, per_head)),
+            pltpu.SemaphoreType.DMA((wo_parts, per_head)),
+            pltpu.SemaphoreType.DMA((4 + wo_parts + n,)),
         ],
         compiler_params=pltpu.CompilerParams(
             collective_id=0, has_side_effects=True, vmem_limit_bytes=60 * 1024 * 1024
@@ -509,7 +600,7 @@
         cost_estimate=pl.CostEstimate(
             flops=flops, bytes_accessed=2 * token_count * width, transcendentals=0
         ),
-    )(tokens, gain, wq, wk, wv, wo, gates, mem_init, norm_init.reshape(kv_heads, 1, HD))
+    )(tokens, gain, wq, wk, wv, wo, gate_bias, mem_init, norm_init.reshape(kv_heads, 1, HD))
 
 
 def solution(mesh):

time: 248 us -> 245 us (0.988)
  Pallas kernels: 243 us -> 240 us
    pallas_call x1, Pallas kernels: 243 us -> 240 us  [per_device(): pl.pallas_call(functools.partial(layer_kernel, n, heads_axis, wo_parts),...]
where the time goes in v2:
time: 245 us; the launch traced here: 243 us
  Pallas kernels  240 us (98%)
  local copies, waits for them, and re-layouts  3.08 us (1%)
    pallas_call x1, Pallas kernels, per_device(): pl.pallas_call(functools.partial(layer_kernel, n, heads_axis, wo_parts),...  240 us

profile of v2, /device:TPU:24, one launch (start us, length us, event | category | flops | bytes accessed | tf_op | source)
XLA Modules:
  0.0 243.0 jit_solution(17795237073724747478)
XLA Ops:
  0.0 239.9 %shard_map.91 = bf16[1024,1024]{1,0:T(8,128)(2,1)} custom-call(bf16[1024,4096]{1,0:T(8,128)(2,1)} %tokens.1, f32[8,1,512]{2,1,0:T(1,128)} %bitcast.2, bf16[512,1024]{1,0:T(8,128)(2,1)} %wq.1, bf16[512,256]{1,0:T(8,128)(2,1)} %wk.1, bf16[512,256]{1,0:T(8,128)(2,1)} %wv.1, bf16[1024,512]{1,0:T(8,128)(2,1)} %wo.1, f32[8]{0:T(128)} %gates.1, ...), custom_call_target="tpu_custom_call" | custom-call | flops 21474836480 | bytes 8388608 | tf_op jit(solution)/shard_map/pallas_call | solution.py:567
  239.9 3.1 %copy.11 = bf16[1024,1024]{1,0:T(8,128)(2,1)} copy(bf16[1024,1024]{1,0:T(8,128)(2,1)} %shard_map.91) | data formatting | bytes 4194304

commit v3 on v2

--- a/solution.py
+++ b/solution.py
@@ -235,15 +235,15 @@
     forward(kv_kind, 1)
     project_hop(acc_kv, kv_columns, kv_kind, 1)
     forward(kv_kind, 2)
+    forward(q_kinds[0], 1)
     middle(acc_kv, kv_columns, kv_kind)
-    forward(q_kinds[0], 1)
+    send_first(q_kinds[1])
     project_hop(acc_kv, kv_columns, kv_kind, hops - 1)
     take_last(kv_kind)
     project(acc_kv, kv_columns, kv_kind, seq_of(pos + hops))
 
     project(acc_q, q_columns[0], q_kinds[0], me, True)
     forward(q_kinds[0], 2)
-    send_first(q_kinds[1])
     project_hop(acc_q, q_columns[0], q_kinds[0], 1)
 
     for j in range(kv_heads):
@@ -269,8 +269,9 @@
         ).astype(jnp.bfloat16)
     send_first(mem_kind)
 
+    forward(q_kinds[1], 1)
     middle(acc_q, q_columns[0], q_kinds[0])
-    forward(q_kinds[1], 1)
+    send_first(wo_kinds[0])
     project_hop(acc_q, q_columns[0], q_kinds[0], hops - 1)
     take_last(q_kinds[0])
     project(acc_q, q_columns[0], q_kinds[0], seq_of(pos + hops))
@@ -324,11 +325,11 @@
     half_heads = q_heads // 2
     round_queries(0)
     forward(q_kinds[1], 2)
-    send_first(wo_kinds[0])
-    forward(mem_kind, 1)
     project(acc_q, q_columns[1], q_kinds[1], me, True)
     project_hop(acc_q, q_columns[1], q_kinds[1], 1)
+    forward(mem_kind, 1)
     lax.fori_loop(0, half_heads // 2, attend, 0)
+    forward(wo_kinds[0], 1)
 
     def q_step(hop, carry):
         forward(q_kinds[1], hop)
@@ -337,26 +338,19 @@
         return carry
 
     lax.fori_loop(3, hops, q_step, 0)
+    if wo_parts > 1:
+        send_first(wo_kinds[1])
     lax.fori_loop(half_heads // 2, half_heads, attend, 0)
-    forward(wo_kinds[0], 1)
-    forward(mem_kind, hops - 1)
     project_hop(acc_q, q_columns[1], q_kinds[1], hops - 1)
     take_last(q_kinds[1])
     project(acc_q, q_columns[1], q_kinds[1], seq_of(pos + hops))
     round_queries(1)
+    lax.fori_loop(half_heads, half_heads + half_heads // 2, attend, 0)
     forward(wo_kinds[0], 2)
+    forward(mem_kind, hops - 1)
+    lax.fori_loop(half_heads + half_heads // 2, q_heads, attend, 0)
     if wo_parts > 1:
-        send_first(wo_kinds[1])
-    lax.fori_loop(half_heads, q_heads, attend, 0)
-
-    def pass_on(kind):
-        def step(hop, carry):
-            forward(kind, hop)
-            return carry
-
-        lax.fori_loop(3, hops, step, 0)
-
-    pass_on(wo_kinds[0])
+        forward(wo_kinds[1], 1)
 
     take_last(mem_kind)
     for j in range(kv_heads):
@@ -460,25 +454,18 @@
                 lax.fori_loop(0, token_count // tile, body, 0)
                 cross(part, c).start()
 
-    def out_hops(part, first, last):
-        def out_step(hop, carry):
-            def emit_side(side, inner):
-                emit(part, seq_of(pos - hop + 2 * hop * side))
-                return inner
-
-            def finish_side(side, inner):
-                finish(part, seq_of(pos - hop + 2 * hop * side))
-                return inner
-
-            lax.fori_loop(0, 2, emit_side, 0)
-            lax.fori_loop(0, 2, finish_side, 0)
+    def each_block(work, part, hop):
+        def side_step(side, carry):
+            work(part, seq_of(pos - hop + 2 * hop * side))
             return carry
 
-        lax.fori_loop(first, last + 1, out_step, 0)
-
-    def out_one(part, c):
-        emit(part, c)
-        finish(part, c)
+        lax.fori_loop(0, 2 - lax.div(1, hop + 1), side_step, 0)
+
+    def emits(part, hop):
+        each_block(emit, part, hop)
+
+    def finishes(part, hop):
+        each_block(finish, part, hop)
 
     def collect(part):
         for o in range(per_head):
@@ -499,20 +486,46 @@
 
             lax.fori_loop(0, token_count // tile, body, 0)
 
-    for part in range(wo_parts):
-        kind = wo_kinds[part]
-        more = part + 1 < wo_parts
-        if more:
-            forward(wo_kinds[part + 1], 1)
-        out_one(part, me)
-        out_hops(part, 1, hops - 2)
-        if more:
-            forward(wo_kinds[part + 1], 2)
-        out_hops(part, hops - 1, hops - 1)
-        take_last(kind)
-        out_one(part, seq_of(pos + hops))
-        if more:
-            pass_on(wo_kinds[part + 1])
+    last_owner = seq_of(pos + hops)
+    two = wo_parts > 1
+    first_kind, second_kind = wo_kinds[0], wo_kinds[-1]
+    emit(0, me)
+    if two:
+        emit(1, me)
+    finish(0, me)
+
+    def out_step(hop, carry):
+        forward(first_kind, hop)
+        emits(0, hop - 2)
+        if two:
+            finishes(1, hop - 3)
+            forward(second_kind, hop - 1)
+            emits(1, hop - 2)
+        finishes(0, hop - 2)
+        return carry
+
+    lax.fori_loop(3, hops, out_step, 0)
+    emits(0, jnp.int32(hops - 2))
+    if two:
+        finishes(1, jnp.int32(hops - 3))
+        forward(second_kind, hops - 1)
+        emits(1, jnp.int32(hops - 2))
+    finishes(0, jnp.int32(hops - 2))
+    emits(0, jnp.int32(hops - 1))
+    if two:
+        finishes(1, jnp.int32(hops - 2))
+    take_last(first_kind)
+    emit(0, last_owner)
+    finishes(0, jnp.int32(hops - 1))
+    if two:
+        emits(1, jnp.int32(hops - 1))
+        finish(0, last_owner)
+        finishes(1, jnp.int32(hops - 1))
+        take_last(second_kind)
+        emit(1, last_owner)
+        finish(1, last_owner)
+    else:
+        finish(0, last_owner)
     for part in range(wo_parts):
         collect(part)
 

time: 245 us -> 259 us (1.057)
  Pallas kernels: 240 us -> 254 us
    pallas_call x1, Pallas kernels: 240 us -> 254 us  [per_device(): pl.pallas_call(functools.partial(layer_kernel, n, heads_axis, wo_parts),...]
where the time goes in v3:
time: 259 us; the launch traced here: 257 us
  Pallas kernels  254 us (98%)
  local copies, waits for them, and re-layouts  3.08 us (1%)
    pallas_call x1, Pallas kernels, per_device(): pl.pallas_call(functools.partial(layer_kernel, n, heads_axis, wo_parts),...  254 us

profile of v3, /device:TPU:24, one launch (start us, length us, event | category | flops | bytes accessed | tf_op | source)
XLA Modules:
  0.0 257.0 jit_solution(8814943897183015507)
XLA Ops:
  0.0 253.9 %shard_map.91 = bf16[1024,1024]{1,0:T(8,128)(2,1)} custom-call(bf16[1024,4096]{1,0:T(8,128)(2,1)} %tokens.1, f32[8,1,512]{2,1,0:T(1,128)} %bitcast.2, bf16[512,1024]{1,0:T(8,128)(2,1)} %wq.1, bf16[512,256]{1,0:T(8,128)(2,1)} %wk.1, bf16[512,256]{1,0:T(8,128)(2,1)} %wv.1, bf16[1024,512]{1,0:T(8,128)(2,1)} %wo.1, f32[8]{0:T(128)} %gates.1, ...), custom_call_target="tpu_custom_call" | custom-call | flops 21474836480 | bytes 8388608 | tf_op jit(solution)/shard_map/pallas_call | solution.py:580
  253.9 3.1 %copy.11 = bf16[1024,1024]{1,0:T(8,128)(2,1)} copy(bf16[1024,1024]{1,0:T(8,128)(2,1)} %shard_map.91) | data formatting | bytes 4194304

commit v4 on v3

--- a/solution.py
+++ b/solution.py
@@ -75,9 +75,7 @@
     block = wo.shape[1]
     sub = block // wo_parts
     tile = 256
-    kv_kind, q_kinds = 0, (1, 2)
-    wo_kinds = tuple(range(3, 3 + wo_parts))
-    mem_kind = 3 + wo_parts
+    kv_kind, q_kind, wo_kind, mem_kind = range(4)
 
     odd = lax.rem(me, 2)
     pos = (1 - odd) * lax.div(me, 2) + odd * (n - 1 - lax.div(me, 2))
@@ -99,13 +97,13 @@
     for part in range(2):
         loads.append(
             pltpu.make_async_copy(
-                wq.at[:, pl.ds(part * q_part, q_part)], q_full.at[part, me], load_sem.at[2 + part]
+                wq.at[:, pl.ds(part * q_part, q_part)], q_full.at[me, part], load_sem.at[2 + part]
             )
         )
     for part in range(wo_parts):
         loads.append(
             pltpu.make_async_copy(
-                wo.at[:, pl.ds(part * sub, sub)], wo_full.at[part, me], load_sem.at[4 + part]
+                wo.at[:, pl.ds(part * sub, sub)], wo_full.at[me, part], load_sem.at[4 + part]
             )
         )
     weight_loads = len(loads)
@@ -125,14 +123,18 @@
         pl.semaphore_signal(barrier, inc=1, device_id=(me, other), device_id_type=MESH)
     pl.semaphore_wait(barrier, 4)
 
-    fulls = [kv_full, q_full.at[0], q_full.at[1]]
-    fulls += [wo_full.at[part] for part in range(wo_parts)]
-    fulls.append(mem_full)
+    fulls = (kv_full, q_full, wo_full, mem_full)
+
+    def part_of(kind, owner, part):
+        if kind == q_kind or (kind == wo_kind and wo_parts == 2):
+            return fulls[kind].at[owner, part]
+        whole = fulls[kind].at[owner, 0] if kind == wo_kind else fulls[kind].at[owner]
+        half = whole.shape[0] // 2
+        return whole.at[pl.ds(part * half, half)]
 
     def ring(kind, way, hop, part):
         owner = seq_of(pos - hop + 1) if way == 0 else seq_of(pos + hop - 1)
-        half = fulls[kind].shape[1] // 2
-        view = fulls[kind].at[owner, pl.ds(part * half, half)]
+        view = part_of(kind, owner, part)
         return pltpu.make_async_remote_copy(
             src_ref=view,
             dst_ref=view,
@@ -144,8 +146,7 @@
 
     def arrival(kind, way, hop, part):
         owner = seq_of(pos - hop) if way == 0 else seq_of(pos + hop)
-        half = fulls[kind].shape[1] // 2
-        view = fulls[kind].at[owner, pl.ds(part * half, half)]
+        view = part_of(kind, owner, part)
         return pltpu.make_async_remote_copy(
             src_ref=view,
             dst_ref=view,
@@ -181,8 +182,9 @@
     loads[1].wait()
     send_first(kv_kind)
     loads[2].wait()
-    send_first(q_kinds[0])
-    for load in loads[3:]:
+    loads[3].wait()
+    send_first(q_kind)
+    for load in loads[4:]:
         load.wait()
 
     def norm_rows(i, carry):
@@ -199,52 +201,42 @@
 
     lax.fori_loop(0, token_count // 64, norm_rows, 0)
 
-    def project(acc, columns, kind, owner, first=False):
+    def project(acc, kind, owner, first=False):
         def body(i, carry):
             rows = pl.ds(pl.multiple_of(i * tile, tile), tile)
-            product = jnp.dot(
-                normed[owner, rows, :], fulls[kind][owner], preferred_element_type=jnp.float32
-            )
-            if first:
-                acc[rows, columns] = product
-            else:
-                acc[rows, columns] += product
+            for part in range(2 if kind == q_kind else 1):
+                weights = fulls[kind][owner, part] if kind == q_kind else fulls[kind][owner]
+                span = weights.shape[-1]
+                columns = slice(part * span, (part + 1) * span)
+                product = jnp.dot(
+                    normed[owner, rows, :], weights, preferred_element_type=jnp.float32
+                )
+                if first:
+                    acc[rows, columns] = product
+                else:
+                    acc[rows, columns] += product
             return carry
 
         lax.fori_loop(0, token_count // tile, body, 0)
 
-    def project_hop(acc, columns, kind, hop):
+    def project_hop(acc, kind, hop):
         def body(side, carry):
-            project(acc, columns, kind, seq_of(pos - hop + 2 * hop * side))
+            project(acc, kind, seq_of(pos - hop + 2 * hop * side))
             return carry
 
         lax.fori_loop(0, 2, body, 0)
 
-    kv_columns = slice(0, 2 * kv_width)
-    q_columns = [slice(part * q_part, (part + 1) * q_part) for part in range(2)]
-
-    def middle(acc, columns, kind):
-        def step(hop, carry):
-            forward(kind, hop)
-            project_hop(acc, columns, kind, hop - 1)
-            return carry
-
-        lax.fori_loop(3, hops, step, 0)
-
-    project(acc_kv, kv_columns, kv_kind, me, True)
-    forward(kv_kind, 1)
-    project_hop(acc_kv, kv_columns, kv_kind, 1)
-    forward(kv_kind, 2)
-    forward(q_kinds[0], 1)
-    middle(acc_kv, kv_columns, kv_kind)
-    send_first(q_kinds[1])
-    project_hop(acc_kv, kv_columns, kv_kind, hops - 1)
+    project(acc_kv, kv_kind, me, True)
+
+    def kv_step(hop, carry):
+        forward(kv_kind, hop)
+        project_hop(acc_kv, kv_kind, hop)
+        return carry
+
+    lax.fori_loop(1, hops, kv_step, 0)
     take_last(kv_kind)
-    project(acc_kv, kv_columns, kv_kind, seq_of(pos + hops))
-
-    project(acc_q, q_columns[0], q_kinds[0], me, True)
-    forward(q_kinds[0], 2)
-    project_hop(acc_q, q_columns[0], q_kinds[0], 1)
+    forward(q_kind, 1)
+    project(acc_kv, kv_kind, seq_of(pos + hops))
 
     for j in range(kv_heads):
         for s in range(segments):
@@ -269,16 +261,22 @@
         ).astype(jnp.bfloat16)
     send_first(mem_kind)
 
-    forward(q_kinds[1], 1)
-    middle(acc_q, q_columns[0], q_kinds[0])
-    send_first(wo_kinds[0])
-    project_hop(acc_q, q_columns[0], q_kinds[0], hops - 1)
-    take_last(q_kinds[0])
-    project(acc_q, q_columns[0], q_kinds[0], seq_of(pos + hops))
-
-    def round_queries(part):
-        for h in range(part * (q_heads // 2), (part + 1) * (q_heads // 2)):
-            queries[h] = acc_q[:, h * HD : (h + 1) * HD].astype(jnp.bfloat16)
+    project(acc_q, q_kind, me, True)
+    project_hop(acc_q, q_kind, 1)
+
+    def q_step(hop, carry):
+        forward(q_kind, hop)
+        forward(mem_kind, hop - 1)
+        project_hop(acc_q, q_kind, hop)
+        return carry
+
+    lax.fori_loop(2, hops, q_step, 0)
+    send_first(wo_kind)
+    forward(mem_kind, hops - 1)
+    take_last(q_kind)
+    project(acc_q, q_kind, seq_of(pos + hops))
+    for h in range(q_heads):
+        queries[h] = acc_q[:, h * HD : (h + 1) * HD].astype(jnp.bfloat16)
 
     exponent_scale = LOG2E / math.sqrt(HD)
     half_seg = SEG // 2
@@ -322,35 +320,9 @@
                 acc_q[start : start + half_seg, columns] = summed / total
         return carry
 
-    half_heads = q_heads // 2
-    round_queries(0)
-    forward(q_kinds[1], 2)
-    project(acc_q, q_columns[1], q_kinds[1], me, True)
-    project_hop(acc_q, q_columns[1], q_kinds[1], 1)
-    forward(mem_kind, 1)
-    lax.fori_loop(0, half_heads // 2, attend, 0)
-    forward(wo_kinds[0], 1)
-
-    def q_step(hop, carry):
-        forward(q_kinds[1], hop)
-        forward(mem_kind, hop - 1)
-        project_hop(acc_q, q_columns[1], q_kinds[1], hop - 1)
-        return carry
-
-    lax.fori_loop(3, hops, q_step, 0)
-    if wo_parts > 1:
-        send_first(wo_kinds[1])
-    lax.fori_loop(half_heads // 2, half_heads, attend, 0)
-    project_hop(acc_q, q_columns[1], q_kinds[1], hops - 1)
-    take_last(q_kinds[1])
-    project(acc_q, q_columns[1], q_kinds[1], seq_of(pos + hops))
-    round_queries(1)
-    lax.fori_loop(half_heads, half_heads + half_heads // 2, attend, 0)
-    forward(wo_kinds[0], 2)
-    forward(mem_kind, hops - 1)
-    lax.fori_loop(half_heads + half_heads // 2, q_heads, attend, 0)
-    if wo_parts > 1:
-        forward(wo_kinds[1], 1)
+    lax.fori_loop(0, q_heads // 2, attend, 0)
+    forward(wo_kind, 1)
+    lax.fori_loop(q_heads // 2, q_heads, attend, 0)
 
     take_last(mem_kind)
     for j in range(kv_heads):
@@ -422,7 +394,7 @@
         def body(i, carry):
             rows = pl.ds(pl.multiple_of(i * tile, tile), tile)
             normed[c, rows, columns] = jnp.dot(
-                mixed[rows, :], wo_full[part, c], preferred_element_type=jnp.float32
+                mixed[rows, :], wo_full[c, part], preferred_element_type=jnp.float32
             ).astype(jnp.bfloat16)
             return carry
 
@@ -461,11 +433,13 @@
 
         lax.fori_loop(0, 2 - lax.div(1, hop + 1), side_step, 0)
 
-    def emits(part, hop):
-        each_block(emit, part, hop)
-
-    def finishes(part, hop):
-        each_block(finish, part, hop)
+    def emits(hop):
+        for part in range(wo_parts):
+            each_block(emit, part, hop)
+
+    def finishes(hop):
+        for part in range(wo_parts):
+            each_block(finish, part, hop)
 
     def collect(part):
         for o in range(per_head):
@@ -487,44 +461,31 @@
             lax.fori_loop(0, token_count // tile, body, 0)
 
     last_owner = seq_of(pos + hops)
-    two = wo_parts > 1
-    first_kind, second_kind = wo_kinds[0], wo_kinds[-1]
-    emit(0, me)
-    if two:
-        emit(1, me)
-    finish(0, me)
+    emits(jnp.int32(0))
+    forward(wo_kind, 2)
+    emits(jnp.int32(1))
+    finishes(jnp.int32(0))
+    emits(jnp.int32(2))
+    finishes(jnp.int32(1))
 
     def out_step(hop, carry):
-        forward(first_kind, hop)
-        emits(0, hop - 2)
-        if two:
-            finishes(1, hop - 3)
-            forward(second_kind, hop - 1)
-            emits(1, hop - 2)
-        finishes(0, hop - 2)
+        finishes(hop - 1)
+        forward(wo_kind, hop)
+        emits(hop)
         return carry
 
     lax.fori_loop(3, hops, out_step, 0)
-    emits(0, jnp.int32(hops - 2))
-    if two:
-        finishes(1, jnp.int32(hops - 3))
-        forward(second_kind, hops - 1)
-        emits(1, jnp.int32(hops - 2))
-    finishes(0, jnp.int32(hops - 2))
-    emits(0, jnp.int32(hops - 1))
-    if two:
-        finishes(1, jnp.int32(hops - 2))
-    take_last(first_kind)
-    emit(0, last_owner)
-    finishes(0, jnp.int32(hops - 1))
-    if two:
-        emits(1, jnp.int32(hops - 1))
-        finish(0, last_owner)
-        finishes(1, jnp.int32(hops - 1))
-        take_last(second_kind)
-        emit(1, last_owner)
-        finish(1, last_owner)
+    if wo_parts == 2:
+        finishes(jnp.int32(hops - 1))
+        for way in range(2):
+            arrival(wo_kind, way, hops, way).wait_recv()
+            emit(way, last_owner)
+        for way in range(2):
+            finish(way, last_owner)
     else:
+        take_last(wo_kind)
+        emit(0, last_owner)
+        finishes(jnp.int32(hops - 1))
         finish(0, last_owner)
     for part in range(wo_parts):
         collect(part)
@@ -570,7 +531,7 @@
     hops = n // 2
     per_head = n // heads_axis
     wo_parts = 2 if block % (2 * HD) == 0 else 1
-    kinds = 4 + wo_parts
+    kinds = 4
     gain = norm_gain.reshape(n, 1, rows_in)
     anywhere = pl.BlockSpec(memory_space=pl.ANY)
     near = pl.BlockSpec(memory_space=pltpu.VMEM)
@@ -585,8 +546,8 @@
         scratch_shapes=[
             pltpu.VMEM((n, token_count, rows_in), bf16),
             pltpu.VMEM((n, rows_in, 2 * kv_width), bf16),
-            pltpu.VMEM((2, n, rows_in, q_width // 2), bf16),
-            pltpu.VMEM((wo_parts, n, q_width, block // wo_parts), bf16),
+            pltpu.VMEM((n, 2, rows_in, q_width // 2), bf16),
+            pltpu.VMEM((n, wo_parts, q_width, block // wo_parts), bf16),
             pltpu.VMEM((n, kv_heads * MEM_ROWS, HD), bf16),
             pltpu.VMEM((token_count, 2 * kv_width), f32),
             pltpu.VMEM((token_count, q_width), f32),

time: 259 us -> 246 us (0.950)
  Pallas kernels: 254 us -> 243 us
    pallas_call x1, Pallas kernels: 254 us -> 243 us  [per_device(): pl.pallas_call(functools.partial(layer_kernel, n, heads_axis, wo_parts),...]
where the time goes in v4:
time: 246 us
  Pallas kernels  243 us (99%)
  local copies, waits for them, and re-layouts  3.08 us (1%)
    pallas_call x1, Pallas kernels, per_device(): pl.pallas_call(functools.partial(layer_kernel, n, heads_axis, wo_parts),...  243 us

profile of v4, /device:TPU:24, one launch (start us, length us, event | category | flops | bytes accessed | tf_op | source)
XLA Modules:
  0.0 246.2 jit_solution(10609787484251300649)
XLA Ops:
  0.0 243.1 %shard_map.91 = bf16[1024,1024]{1,0:T(8,128)(2,1)} custom-call(bf16[1024,4096]{1,0:T(8,128)(2,1)} %tokens.1, f32[8,1,512]{2,1,0:T(1,128)} %bitcast.2, bf16[512,1024]{1,0:T(8,128)(2,1)} %wq.1, bf16[512,256]{1,0:T(8,128)(2,1)} %wk.1, bf16[512,256]{1,0:T(8,128)(2,1)} %wv.1, bf16[1024,512]{1,0:T(8,128)(2,1)} %wo.1, f32[8]{0:T(128)} %gates.1, ...), custom_call_target="tpu_custom_call" | custom-call | flops 21474836480 | bytes 8388608 | tf_op jit(solution)/shard_map/pallas_call | solution.py:541
  243.1 3.1 %copy.11 = bf16[1024,1024]{1,0:T(8,128)(2,1)} copy(bf16[1024,1024]{1,0:T(8,128)(2,1)} %shard_map.91) | data formatting | bytes 4194304

commit v5 on v4

--- a/solution.py
+++ b/solution.py
@@ -49,11 +49,14 @@
     memory,
     mixed,
     got,
+    far,
     xgot,
     ring_send,
     ring_recv,
     give_send,
     give_recv,
+    far_send,
+    far_recv,
     x_send,
     x_recv,
     load_sem,
@@ -88,7 +91,8 @@
     sides = (seq_of(pos + 1), seq_of(pos - 1))
     core = lax.rem(head, 2)
     partner = head + 1 - 2 * core
-    across = lax.rem(head + heads_axis // 2, heads_axis)
+    chip = lax.div(head, 2)
+    others = [lax.rem(head + 2 + i - core, heads_axis) for i in range(2)]
 
     loads = [
         pltpu.make_async_copy(wk, kv_full.at[me, :, pl.ds(0, kv_width)], load_sem.at[0]),
@@ -119,9 +123,9 @@
     barrier = pltpu.get_barrier_semaphore()
     for side in sides:
         pl.semaphore_signal(barrier, inc=1, device_id=(side, head), device_id_type=MESH)
-    for other in (partner, across):
+    for other in (partner, others[0], others[1]):
         pl.semaphore_signal(barrier, inc=1, device_id=(me, other), device_id_type=MESH)
-    pl.semaphore_wait(barrier, 4)
+    pl.semaphore_wait(barrier, 5)
 
     fulls = (kv_full, q_full, wo_full, mem_full)
 
@@ -361,18 +365,30 @@
 
     lax.fori_loop(0, q_heads, retrieve, 0)
 
-    def place_of(c):
-        target = lax.div(c, per_head)
-        slot = lax.div(target, 2) * per_head + lax.rem(c, per_head)
-        return target, slot
-
-    def give(part, c):
-        target, slot = place_of(c)
+    def summer_of(part, c):
+        return part if wo_parts == 2 else lax.rem(lax.rem(c, per_head), 2)
+
+    def far_slot(c):
+        return lax.rem(lax.div(c, per_head), 2) * per_head + lax.rem(c, per_head)
+
+    def give_home(part, c):
+        index = lax.rem(c, per_head)
         return pltpu.make_async_remote_copy(
             src_ref=normed.at[c, :, pl.ds(part * sub, sub)],
-            dst_ref=got.at[part, slot],
-            send_sem=give_send.at[part, slot],
-            recv_sem=give_recv.at[part, slot],
+            dst_ref=got.at[part, index],
+            send_sem=give_send.at[part, index],
+            recv_sem=give_recv.at[part, index],
+            device_id=(me, partner),
+            device_id_type=MESH,
+        )
+
+    def give_far(part, c):
+        slot = far_slot(c)
+        return pltpu.make_async_remote_copy(
+            src_ref=normed.at[c, :, pl.ds(part * sub, sub)],
+            dst_ref=far.at[slot],
+            send_sem=far_send.at[slot],
+            recv_sem=far_recv.at[slot],
             device_id=(me, partner),
             device_id_type=MESH,
         )
@@ -382,11 +398,28 @@
         return pltpu.make_async_remote_copy(
             src_ref=normed.at[c, :, pl.ds(part * sub, sub)],
             dst_ref=xgot.at[part, index],
-            send_sem=x_send.at[part, index],
+            send_sem=x_send.at[far_slot(c)],
             recv_sem=x_recv.at[part, index],
-            device_id=(me, across),
+            device_id=(me, lax.div(c, per_head)),
             device_id_type=MESH,
         )
+
+    def cross_arrival(part, c):
+        index = lax.rem(c, per_head)
+        return pltpu.make_async_remote_copy(
+            src_ref=normed.at[c, :, pl.ds(part * sub, sub)],
+            dst_ref=xgot.at[part, index],
+            send_sem=x_send.at[far_slot(c)],
+            recv_sem=x_recv.at[part, index],
+            device_id=(me, others[0]),
+            device_id_type=MESH,
+        )
+
+    def roles(part, c):
+        target = lax.div(c, per_head)
+        away = lax.div(target, 2) != chip
+        mine = summer_of(part, c) == core
+        return target, away, mine
 
     def emit(part, c):
         columns = slice(part * sub, (part + 1) * sub)
@@ -399,32 +432,35 @@
             return carry
 
         lax.fori_loop(0, token_count // tile, body, 0)
-        target, slot = place_of(c)
-
-        @pl.when(lax.rem(target, 2) != core)
+        target, away, mine = roles(part, c)
+
+        @pl.when(away & jnp.logical_not(mine))
         def _():
-            give(part, c).start()
+            give_far(part, c).start()
+
+        @pl.when(target == partner)
+        def _():
+            give_home(part, c).start()
 
     def finish(part, c):
-        target, slot = place_of(c)
+        target, away, mine = roles(part, c)
         columns = slice(part * sub, (part + 1) * sub)
-
-        @pl.when(lax.rem(target, 2) == core)
+        slot = far_slot(c)
+
+        @pl.when(away & mine)
         def _():
-            give(part, c).wait_recv()
+            give_far(part, c).wait_recv()
 
             def body(i, carry):
                 rows = pl.ds(pl.multiple_of(i * tile, tile), tile)
                 normed[c, rows, columns] = (
                     normed[c, rows, columns].astype(jnp.float32)
-                    + got[part, slot, rows, :].astype(jnp.float32)
+                    + far[slot, rows, :].astype(jnp.float32)
                 ).astype(jnp.bfloat16)
                 return carry
 
-            @pl.when(target != head)
-            def _():
-                lax.fori_loop(0, token_count // tile, body, 0)
-                cross(part, c).start()
+            lax.fori_loop(0, token_count // tile, body, 0)
+            cross(part, c).start()
 
     def each_block(work, part, hop):
         def side_step(side, carry):
@@ -444,8 +480,8 @@
     def collect(part):
         for o in range(per_head):
             c = head * per_head + o
-            cross(part, c).wait_recv()
-            slot = lax.div(head, 2) * per_head + o
+            give_home(part, c).wait_recv()
+            cross_arrival(part, c).wait_recv()
             columns = slice(part * sub, (part + 1) * sub)
             placed = slice(o * block + part * sub, o * block + (part + 1) * sub)
 
@@ -453,7 +489,7 @@
                 rows = pl.ds(pl.multiple_of(i * tile, tile), tile)
                 out[rows, placed] = (
                     normed[c, rows, columns].astype(jnp.float32)
-                    + got[part, slot, rows, :].astype(jnp.float32)
+                    + got[part, o, rows, :].astype(jnp.float32)
                     + xgot[part, o, rows, :].astype(jnp.float32)
                 ).astype(jnp.bfloat16)
                 return carry
@@ -503,14 +539,18 @@
             ring(kind, way, hops, way).wait_send()
 
     def drain_out(c, carry):
-        target, slot = place_of(c)
         for part in range(wo_parts):
-
-            @pl.when(lax.rem(target, 2) != core)
+            target, away, mine = roles(part, c)
+
+            @pl.when(away & jnp.logical_not(mine))
             def _():
-                give(part, c).wait_send()
-
-            @pl.when((lax.rem(target, 2) == core) & (target != head))
+                give_far(part, c).wait_send()
+
+            @pl.when(target == partner)
+            def _():
+                give_home(part, c).wait_send()
+
+            @pl.when(away & mine)
             def _():
                 cross(part, c).wait_send()
 
@@ -558,13 +598,16 @@
             pltpu.VMEM((segments, kv_heads, 8, HD), f32),
             pltpu.VMEM((segments, kv_heads, HD, 2 * HD), bf16),
             pltpu.VMEM((token_count, q_width), bf16),
-            pltpu.VMEM((wo_parts, n // 2, token_count, block // wo_parts), bf16),
+            pltpu.VMEM((wo_parts, per_head, token_count, block // wo_parts), bf16),
+            pltpu.VMEM((2 * per_head, token_count, block // wo_parts), bf16),
             pltpu.VMEM((wo_parts, per_head, token_count, block // wo_parts), bf16),
             pltpu.SemaphoreType.DMA((kinds, 2, hops, 2)),
             pltpu.SemaphoreType.DMA((kinds, 2, hops, 2)),
-            pltpu.SemaphoreType.DMA((wo_parts, n // 2)),
-            pltpu.SemaphoreType.DMA((wo_parts, n // 2)),
             pltpu.SemaphoreType.DMA((wo_parts, per_head)),
+            pltpu.SemaphoreType.DMA((wo_parts, per_head)),
+            pltpu.SemaphoreType.DMA((2 * per_head,)),
+            pltpu.SemaphoreType.DMA((2 * per_head,)),
+            pltpu.SemaphoreType.DMA((2 * per_head,)),
             pltpu.SemaphoreType.DMA((wo_parts, per_head)),
             pltpu.SemaphoreType.DMA((4 + wo_parts + n,)),
         ],

time: 246 us -> 249 us (1.012)
  no operation moved by 1% of the time
where the time goes in v5:
time: 249 us; the launch traced here: 248 us
  Pallas kernels  245 us (98%)
  local copies, waits for them, and re-layouts  3.08 us (1%)
    pallas_call x1, Pallas kernels, per_device(): pl.pallas_call(functools.partial(layer_kernel, n, heads_axis, wo_parts),...  245 us

profile of v5, /device:TPU:24, one launch (start us, length us, event | category | flops | bytes accessed | tf_op | source)
XLA Modules:
  0.0 247.8 jit_solution(13291949198421518183)
XLA Ops:
  0.0 244.8 %shard_map.91 = bf16[1024,1024]{1,0:T(8,128)(2,1)} custom-call(bf16[1024,4096]{1,0:T(8,128)(2,1)} %tokens.1, f32[8,1,512]{2,1,0:T(1,128)} %bitcast.2, bf16[512,1024]{1,0:T(8,128)(2,1)} %wq.1, bf16[512,256]{1,0:T(8,128)(2,1)} %wk.1, bf16[512,256]{1,0:T(8,128)(2,1)} %wv.1, bf16[1024,512]{1,0:T(8,128)(2,1)} %wo.1, f32[8]{0:T(128)} %gates.1, ...), custom_call_target="tpu_custom_call" | custom-call | flops 21474836480 | bytes 8388608 | tf_op jit(solution)/shard_map/pallas_call | solution.py:581
  244.8 3.1 %copy.11 = bf16[1024,1024]{1,0:T(8,128)(2,1)} copy(bf16[1024,1024]{1,0:T(8,128)(2,1)} %shard_map.91) | data formatting | bytes 4194304

commit v6 on v2

--- a/solution.py
+++ b/solution.py
@@ -509,12 +509,13 @@
         if more:
             forward(wo_kinds[part + 1], 2)
         out_hops(part, hops - 1, hops - 1)
+        if part:
+            collect(part - 1)
         take_last(kind)
         out_one(part, seq_of(pos + hops))
         if more:
             pass_on(wo_kinds[part + 1])
-    for part in range(wo_parts):
-        collect(part)
+    collect(wo_parts - 1)
 
     for kind in range(len(fulls)):
 

time: 245 us -> 245 us (level)
  no operation moved by 1% of the time
where the time goes in v6:
time: 245 us; the launch traced here: 243 us
  Pallas kernels  240 us (98%)
  local copies, waits for them, and re-layouts  3.08 us (1%)
    pallas_call x1, Pallas kernels, per_device(): pl.pallas_call(functools.partial(layer_kernel, n, heads_axis, wo_parts),...  240 us

profile of v6, /device:TPU:24, one launch (start us, length us, event | category | flops | bytes accessed | tf_op | source)
XLA Modules:
  0.0 243.0 jit_solution(15404579641724172040)
XLA Ops:
  0.0 239.9 %shard_map.91 = bf16[1024,1024]{1,0:T(8,128)(2,1)} custom-call(bf16[1024,4096]{1,0:T(8,128)(2,1)} %tokens.1, f32[8,1,512]{2,1,0:T(1,128)} %bitcast.2, bf16[512,1024]{1,0:T(8,128)(2,1)} %wq.1, bf16[512,256]{1,0:T(8,128)(2,1)} %wk.1, bf16[512,256]{1,0:T(8,128)(2,1)} %wv.1, bf16[1024,512]{1,0:T(8,128)(2,1)} %wo.1, f32[8]{0:T(128)} %gates.1, ...), custom_call_target="tpu_custom_call" | custom-call | flops 21474836480 | bytes 8388608 | tf_op jit(solution)/shard_map/pallas_call | solution.py:568
  239.9 3.1 %copy.11 = bf16[1024,1024]{1,0:T(8,128)(2,1)} copy(bf16[1024,1024]{1,0:T(8,128)(2,1)} %shard_map.91) | data formatting | bytes 4194304
